TPU v7x, 512 devices: a whole 4x4x16 slice. The times are simulated.
512 devices in a mesh: grp: 32 (over x, y, core), tp: 16 (over z).
Axes of the slice: x: 4, y: 4, z: 16, core: 2. Of those that a mesh axis runs over, the one named last changes fastest.
Arguments:
- queries: bfloat16 [32, 2048, 2048], P('grp', 'tp'), may hold values from -6 to 6
- keys: bfloat16 [32, 2048, 2048], P('grp', 'tp'), may hold values from -6 to 6
- values: bfloat16 [32, 2048, 2048], P('grp', 'tp'), may hold values from -6 to 6
- upstream: bfloat16 [32, 2048, 2048], P('grp', 'tp'), may hold values from -6 to 6
- q_gain: float32 [128], replicated, may hold values from 0.5 to 1.5
- k_gain: float32 [128], replicated, may hold values from 0.5 to 1.5
- segments: int32 [32, 2048], P('grp'), may hold values from 0 to 31, never falling along the last dimension, each value on 1 to 128 neighbouring positions
Outputs:
- attended: bfloat16 [32, 2048, 2048], P('grp', 'tp')
- query_grad: bfloat16 [32, 2048, 2048], P('grp', 'tp')
- key_grad: bfloat16 [32, 2048, 2048], P('grp', 'tp')
- value_grad: bfloat16 [32, 2048, 2048], P('grp', 'tp')
- gain_grads: float32 [2, 128], replicated
Inputs may be any that keep to these rules, and one draw needn't show every extreme that they name: In each sequence segment numbers never fall, each of the 32 segments occupies 1 to 128 positions, and some segment occupies exactly 128.
All inputs are finite; a program needn't handle non-finite values.
Results may differ from a plain program's by a relative error of at most 0.012.
Values may be sent and summed in bfloat16 or wider, within the bound.
No kernel may reach another device: no remote copies, remote signals or barrier semaphores. Data moves between devices by JAX's collectives and lax.ppermute only.
A program may use at most 64 MiB of HBM per device.

v0:
```python
import math

import jax
import jax.numpy as jnp
from jax import lax
from jax.sharding import PartitionSpec as P


def normalize(block, gain):
    values_f = block.astype(jnp.float32)
    recip = lax.rsqrt(jnp.mean(values_f * values_f, axis=-1, keepdims=True) + 1e-06)
    unit = values_f * recip
    return (unit, recip, (unit * gain).astype(jnp.bfloat16))


def norm_back(unit, recip, normgrad, gain):
    scaled = normgrad * gain
    inner = jnp.mean(scaled * unit, axis=-1, keepdims=True)
    return (recip * (scaled - unit * inner)).astype(jnp.bfloat16)


def attend(query_h, key_h, value_h, grad_h, query_seg, key_seg, scale):
    scores = jnp.einsum("qhd,khd->hqk", query_h, key_h, preferred_element_type=jnp.float32) * scale
    same = (query_seg[:, None] == key_seg[None, :])[None]
    weight = jnp.where(same, jnp.exp(scores), 0.0)
    probs = weight / jnp.sum(weight, axis=-1, keepdims=True)
    rounded = probs.astype(jnp.bfloat16)
    output = jnp.einsum("hqk,khd->qhd", rounded, value_h, preferred_element_type=jnp.float32)
    dprobs = jnp.einsum("qhd,khd->hqk", grad_h, value_h, preferred_element_type=jnp.float32)
    delta = jnp.einsum("qhd,qhd->hq", grad_h.astype(jnp.float32), output)[..., None]
    dscores = (probs * (dprobs - delta)).astype(jnp.bfloat16)
    dquery = jnp.einsum("hqk,khd->qhd", dscores, key_h, preferred_element_type=jnp.float32) * scale
    dkey = jnp.einsum("hqk,qhd->khd", dscores, query_h, preferred_element_type=jnp.float32) * scale
    dvalue = jnp.einsum("hqk,qhd->khd", rounded, grad_h, preferred_element_type=jnp.float32)
    return (output, dquery, dkey, dvalue)


def per_device(queries, keys, values, upstream, q_gain, k_gain, segments):
    rows = queries.shape[1]
    head_dim = q_gain.shape[0]
    heads = queries.shape[2] // head_dim
    shape3 = (rows, heads, head_dim)
    scale = 1.0 / math.sqrt(head_dim)
    q_unit, q_recip, q_norm = normalize(queries[0].reshape(shape3), q_gain)
    k_unit, k_recip, k_norm = normalize(keys[0].reshape(shape3), k_gain)
    value3 = values[0].reshape(shape3)
    grad3 = upstream[0].reshape(shape3)
    seq_ids = segments[0]
    total = seq_ids.shape[0]
    q_heads, k_heads, v_heads, g_heads = (
        lax.all_to_all(q_norm, "tp", split_axis=1, concat_axis=0, tiled=True),
        lax.all_to_all(k_norm, "tp", split_axis=1, concat_axis=0, tiled=True),
        lax.all_to_all(value3, "tp", split_axis=1, concat_axis=0, tiled=True),
        lax.all_to_all(grad3, "tp", split_axis=1, concat_axis=0, tiled=True),
    )
    block = min(512, total)
    local_heads = q_heads.shape[1]
    empty = jnp.zeros((total, local_heads, head_dim), jnp.float32)

    def step(index, carry):
        out_acc, dq_acc, dk_acc, dv_acc = carry
        start = index * block
        q_block = lax.dynamic_slice_in_dim(q_heads, start, block, 0)
        g_block = lax.dynamic_slice_in_dim(g_heads, start, block, 0)
        query_seg = lax.dynamic_slice_in_dim(seq_ids, start, block, 0)
        output, dquery, dkey, dvalue = attend(
            q_block, k_heads, v_heads, g_block, query_seg, seq_ids, scale
        )
        out_acc = lax.dynamic_update_slice_in_dim(out_acc, output, start, 0)
        dq_acc = lax.dynamic_update_slice_in_dim(dq_acc, dquery, start, 0)
        dk_acc = dk_acc + dkey
        dv_acc = dv_acc + dvalue
        return (out_acc, dq_acc, dk_acc, dv_acc)

    out_all, dq_all, dk_all, dv_all = lax.fori_loop(
        0, total // block, step, (empty, empty, empty, empty)
    )
    out_rows, dv_rows = (
        lax.all_to_all(out_all.astype(jnp.bfloat16), "tp", split_axis=0, concat_axis=1, tiled=True),
        lax.all_to_all(dv_all.astype(jnp.bfloat16), "tp", split_axis=0, concat_axis=1, tiled=True),
    )
    q_normgrad, k_normgrad = (
        lax.all_to_all(dq_all, "tp", split_axis=0, concat_axis=1, tiled=True),
        lax.all_to_all(dk_all, "tp", split_axis=0, concat_axis=1, tiled=True),
    )
    query_grad = norm_back(q_unit, q_recip, q_normgrad, q_gain)
    key_grad = norm_back(k_unit, k_recip, k_normgrad, k_gain)
    partial_sums = jnp.stack(
        [jnp.sum(q_normgrad * q_unit, axis=(0, 1)), jnp.sum(k_normgrad * k_unit, axis=(0, 1))]
    )
    count_all = lax.axis_size("grp") * total * heads
    gain_grads = lax.psum(partial_sums, ("grp", "tp")) * (1.0 / math.sqrt(count_all))
    flat = (1, rows, heads * head_dim)
    return (
        out_rows.reshape(flat),
        query_grad.reshape(flat),
        key_grad.reshape(flat),
        dv_rows.reshape(flat),
        gain_grads,
    )


def solution(mesh):
    in_specs = (
        P("grp", "tp", None),
        P("grp", "tp", None),
        P("grp", "tp", None),
        P("grp", "tp", None),
        P(),
        P(),
        P("grp", None),
    )
    out_specs = (
        P("grp", "tp", None),
        P("grp", "tp", None),
        P("grp", "tp", None),
        P("grp", "tp", None),
        P(),
    )
    return jax.shard_map(
        per_device, mesh=mesh, in_specs=in_specs, out_specs=out_specs, check_vma=False
    )
```

profile of v0, /device:TPU:1, one launch (start us, length us, event | category | flops | bytes accessed | tf_op | source)
XLA Modules:
  0.0 509.5 jit_solution(13366239089425066338)
XLA Ops:
  0.7 1.4 copy.86
  2.2 1.6 multiply_convert_fusion.2
  3.9 15.7 %all-to-all-start = ((bf16[128,16,128]{0,2,1:T(8,128)(2,1)}), bf16[128,16,128]{0,2,1:T(8,128)(2,1)S(1)}, u32[]{:S(2)}, u32[]{:S(2)}) async-start(bf16[128,16,128]{0,2,1:T(8,128)(2,1)} %multiply_convert_fusion.2), calls=%async_computation | async-start | bytes 1048576 | tf_op jit(solution)/shard_map/all_to_all | solution.py:51
  22.0 20.4 %all-to-all-done = bf16[128,16,128]{0,2,1:T(8,128)(2,1)S(1)} async-done(((bf16[128,16,128]{0,2,1:T(8,128)(2,1)}), bf16[128,16,128]{0,2,1:T(8,128)(2,1)S(1)}, u32[]{:S(2)}, u32[]{:S(2)}) %all-to-all-start) | async-done | bytes 524320 | tf_op jit(solution)/shard_map/all_to_all | solution.py:51
  42.4 12.6 %all-to-all-start.1 = ((bf16[128,16,128]{0,2,1:T(8,128)(2,1)}), bf16[128,16,128]{0,2,1:T(8,128)(2,1)S(1)}, u32[]{:S(2)}, u32[]{:S(2)}) async-start(bf16[128,16,128]{0,2,1:T(8,128)(2,1)} %multiply_convert_fusion.1), calls=%async_computation.1 | async-start | bytes 1048576 | tf_op jit(solution)/shard_map/all_to_all | solution.py:52
  56.0 21.8 %all-to-all-done.1 = bf16[128,16,128]{0,2,1:T(8,128)(2,1)S(1)} async-done(((bf16[128,16,128]{0,2,1:T(8,128)(2,1)}), bf16[128,16,128]{0,2,1:T(8,128)(2,1)S(1)}, u32[]{:S(2)}, u32[]{:S(2)}) %all-to-all-start.1) | async-done | bytes 524320 | tf_op jit(solution)/shard_map/all_to_all | solution.py:52
  77.8 12.6 %all-to-all-start.2 = ((bf16[128,16,128]{0,2,1:T(8,128)(2,1)}), bf16[128,16,128]{0,2,1:T(8,128)(2,1)S(1)}, u32[]{:S(2)}, u32[]{:S(2)}) async-start(bf16[128,16,128]{0,2,1:T(8,128)(2,1)} %bitcast.198), calls=%async_computation.2 | async-start | bytes 1048576 | tf_op jit(solution)/shard_map/all_to_all | solution.py:53
  90.5 2.0 copy.92
  92.5 20.7 %all-to-all-done.2 = bf16[128,16,128]{0,2,1:T(8,128)(2,1)S(1)} async-done(((bf16[128,16,128]{0,2,1:T(8,128)(2,1)}), bf16[128,16,128]{0,2,1:T(8,128)(2,1)S(1)}, u32[]{:S(2)}, u32[]{:S(2)}) %all-to-all-start.2) | async-done | bytes 524320 | tf_op jit(solution)/shard_map/all_to_all | solution.py:53
  113.3 12.7 %all-to-all-start.3 = ((bf16[128,16,128]{0,2,1:T(8,128)(2,1)}), bf16[128,16,128]{0,2,1:T(8,128)(2,1)}, u32[]{:S(2)}, u32[]{:S(2)}) async-start(bf16[128,16,128]{0,2,1:T(8,128)(2,1)} %bitcast.197), calls=%async_computation.3 | async-start | bytes 1048576 | tf_op jit(solution)/shard_map/all_to_all | solution.py:54
  127.1 1.3 copy.89
  128.4 2.0 copy.91
  130.5 18.4 %all-to-all-done.3 = bf16[128,16,128]{0,2,1:T(8,128)(2,1)} async-done(((bf16[128,16,128]{0,2,1:T(8,128)(2,1)}), bf16[128,16,128]{0,2,1:T(8,128)(2,1)}, u32[]{:S(2)}, u32[]{:S(2)}) %all-to-all-start.3) | async-done | bytes 524320 | tf_op jit(solution)/shard_map/all_to_all | solution.py:54
  148.8 2.0 copy.93
  150.9 1.1 broadcast_in_dim.29
  152.0 47.6 %while.20 = (s32[]{:T(128)}, bf16[2048,1,128]{2,0,1:T(8,128)(2,1)}, f32[2048,1,128]{2,0,1:T(8,128)}, f32[2048,1,128]{0,2,1:T(8,128)S(1)}, f32[2048,1,128]{0,2,1:...) while((s32[]{:T(128)}, bf16[2048,1,128]{2,0,1:T(8,128)(2,1)}, ...), condition=%wide.region_4.5_spmd.clone, body=%wide.region_2.4_spmd.clone.sunk | while | flops 1624767488 | bytes 56256876 | solution.py:75
  152.0 3.0 fusion.61
  155.0 3.9 fusion.65
  162.2 1.4 fusion.63
  163.7 3.0 fusion.61
  166.7 4.2 fusion.65
  174.1 1.5 fusion.63
  175.7 3.0 fusion.61
  178.7 4.2 fusion.65
  186.1 1.4 fusion.63
  187.6 3.0 fusion.61
  190.6 4.2 fusion.65
  198.1 1.5 fusion.63
  199.5 1.3 convert_element_type.76
  201.4 1.7 reduce.7
  203.1 1.3 copy.114
  205.3 12.7 %all-to-all-start.7 = ((bf16[16,2,8192]{2,1,0:T(2,128)(2,1)}), bf16[16,2,8192]{2,1,0:T(2,128)(2,1)S(1)}, u32[]{:S(2)}, u32[]{:S(2)}) async-start(bf16[16,2,8192]{2,1,0:T(2,128)(2,1)} %reshape.220), calls=%async_computation.7 | async-start | bytes 1048576 | tf_op jit(solution)/shard_map/all_to_all | solution.py:80
  218.0 1.7 reduce.6
  219.6 2.0 reshape.218
  221.6 19.2 %all-to-all-done.7 = bf16[16,2,8192]{2,1,0:T(2,128)(2,1)S(1)} async-done(((bf16[16,2,8192]{2,1,0:T(2,128)(2,1)}), bf16[16,2,8192]{2,1,0:T(2,128)(2,1)S(1)}, u32[]{:S(2)}, u32[]{:S(2)}) %all-to-all-start.7) | async-done | bytes 524320 | tf_op jit(solution)/shard_map/all_to_all | solution.py:80
  240.8 12.7 %all-to-all-start.4 = ((bf16[16,2,8192]{2,1,0:T(2,128)(2,1)}), bf16[16,2,8192]{2,1,0:T(2,128)(2,1)}, u32[]{:S(2)}, u32[]{:S(2)}) async-start(bf16[16,2,8192]{2,1,0:T(2,128)(2,1)} %reshape.218), calls=%async_computation.4 | async-start | bytes 1048576 | tf_op jit(solution)/shard_map/all_to_all | solution.py:79
  254.2 22.2 %all-to-all-done.4 = bf16[16,2,8192]{2,1,0:T(2,128)(2,1)} async-done(((bf16[16,2,8192]{2,1,0:T(2,128)(2,1)}), bf16[16,2,8192]{2,1,0:T(2,128)(2,1)}, u32[]{:S(2)}, u32[]{:S(2)}) %all-to-all-start.4) | async-done | bytes 524320 | tf_op jit(solution)/shard_map/all_to_all | solution.py:79
  276.4 57.9 %all_to_all.144 = f32[2048,1,128]{2,1,0:T(1,128)} all-to-all(f32[2048,1,128]{2,1,0:T(1,128)S(1)} %copy.98), channel_id=1, replica_groups=mesh['grp'=32,'tp'=16] {'tp'}, dimensions={0} | all-to-all | bytes 2097152 | tf_op jit(solution)/shard_map/all_to_all | solution.py:84
  334.3 12.7 %all-to-all-start.5 = ((f32[2048,1,128]{2,1,0:T(1,128)}), f32[2048,1,128]{2,1,0:T(1,128)}, u32[]{:S(2)}, u32[]{:S(2)}) async-start(f32[2048,1,128]{2,1,0:T(1,128)} %bitcast.20), calls=%async_computation.5 | async-start | bytes 2097152 | tf_op jit(solution)/shard_map/all_to_all | solution.py:83
  347.1 2.2 reshape.221
  350.7 2.2 reshape.219
  353.8 1.3 copy.95
  356.1 1.6 copy.99
  358.0 34.2 %all-to-all-done.5 = f32[2048,1,128]{2,1,0:T(1,128)} async-done(((f32[2048,1,128]{2,1,0:T(1,128)}), f32[2048,1,128]{2,1,0:T(1,128)}, u32[]{:S(2)}, u32[]{:S(2)}) %all-to-all-start.5) | async-done | bytes 1048608 | tf_op jit(solution)/shard_map/all_to_all | solution.py:83
  392.3 1.6 copy.97
  394.2 109.7 %psum.7 = f32[2,128]{1,0:T(2,128)S(1)} all-reduce(f32[2,128]{1,0:T(2,128)S(1)} %pad_maximum_fusion), channel_id=1, replica_groups=mesh['grp'=32,'tp'=16] {'grp','tp'}, use_global_device_ids=true, to_apply=%region_9.10 | all-reduce | flops 256 | bytes 2048 | tf_op jit(solution)/shard_map/psum | solution.py:92
  504.4 1.5 fusion.30
  506.9 1.5 fusion.27
  (115 shorter events, 26.3 us)
Async XLA Ops:
  0.6 19.0 %copy-start.11 = (bf16[1,128,2048]{2,1,0:T(8,128)(2,1)S(1)}, bf16[1,128,2048]{2,1,0:T(8,128)(2,1)}, u32[]{:S(2)}) copy-start(bf16[1,128,2048]{2,1,0:T(8,128)(2,1)} %param.10) | copy-start | bytes 1572868
  0.6 20.4 %copy-start.15 = (f32[128]{0:T(128)S(1)}, f32[128]{0:T(128)}, u32[]{:S(2)}) copy-start(f32[128]{0:T(128)} %param.14) | copy-start | bytes 1540
  2.0 20.0 %copy-start.2 = (bf16[1,128,2048]{1,2,0:T(8,128)(2,1)}, bf16[1,128,2048]{1,2,0:T(8,128)(2,1)S(1)}, u32[]{:S(2)}) copy-start(bf16[1,128,2048]{1,2,0:T(8,128)(2,1)S(1)} %copy.86) | copy-start | bytes 1572868
  3.9 38.6 %all-to-all-start = ((bf16[128,16,128]{0,2,1:T(8,128)(2,1)}), bf16[128,16,128]{0,2,1:T(8,128)(2,1)S(1)}, u32[]{:S(2)}, u32[]{:S(2)}) async-start(bf16[128,16,128]{0,2,1:T(8,128)(2,1)} %multiply_convert_fusion.2), calls=%async_computation | async-start | bytes 1048576 | tf_op jit(solution)/shard_map/all_to_all | solution.py:51
  19.9 93.4 %copy-start.3 = (bf16[1,128,2048]{1,2,0:T(8,128)(2,1)}, bf16[1,128,2048]{1,2,0:T(8,128)(2,1)S(1)}, u32[]{:S(2)}) copy-start(bf16[1,128,2048]{1,2,0:T(8,128)(2,1)S(1)} %copy.88) | copy-start | bytes 1572868
  19.9 35.1 %copy-start.12 = (bf16[1,128,2048]{2,1,0:T(8,128)(2,1)S(1)}, bf16[1,128,2048]{2,1,0:T(8,128)(2,1)}, u32[]{:S(2)}) copy-start(bf16[1,128,2048]{2,1,0:T(8,128)(2,1)} %param.11) | copy-start | bytes 1572868
  20.1 1.0 copy-start
  42.4 35.4 %all-to-all-start.1 = ((bf16[128,16,128]{0,2,1:T(8,128)(2,1)}), bf16[128,16,128]{0,2,1:T(8,128)(2,1)S(1)}, u32[]{:S(2)}, u32[]{:S(2)}) async-start(bf16[128,16,128]{0,2,1:T(8,128)(2,1)} %multiply_convert_fusion.1), calls=%async_computation.1 | async-start | bytes 1048576 | tf_op jit(solution)/shard_map/all_to_all | solution.py:52
  77.8 35.4 %copy-start.6 = (bf16[128,16,128]{0,2,1:T(8,128)(2,1)}, bf16[128,16,128]{0,2,1:T(8,128)(2,1)S(1)}, u32[]{:S(2)}) copy-start(bf16[128,16,128]{0,2,1:T(8,128)(2,1)S(1)} %all-to-all-done.1) | copy-start | bytes 1572868
  77.8 35.4 %all-to-all-start.2 = ((bf16[128,16,128]{0,2,1:T(8,128)(2,1)}), bf16[128,16,128]{0,2,1:T(8,128)(2,1)S(1)}, u32[]{:S(2)}, u32[]{:S(2)}) async-start(bf16[128,16,128]{0,2,1:T(8,128)(2,1)} %bitcast.198), calls=%async_computation.2 | async-start | bytes 1048576 | tf_op jit(solution)/shard_map/all_to_all | solution.py:53
  90.5 61.5 %copy-start.14 = (s32[1,2048]{1,0:T(1,128)S(1)}, s32[1,2048]{1,0:T(1,128)}, u32[]{:S(2)}) copy-start(s32[1,2048]{1,0:T(1,128)} %param.15) | copy-start | bytes 24580
  113.3 13.6 %copy-start.10 = (bf16[128,16,128]{0,2,1:T(8,128)(2,1)}, bf16[128,16,128]{0,2,1:T(8,128)(2,1)S(1)}, u32[]{:S(2)}) copy-start(bf16[128,16,128]{0,2,1:T(8,128)(2,1)S(1)} %all-to-all-done.2) | copy-start | bytes 1572868
  113.3 35.6 %all-to-all-start.3 = ((bf16[128,16,128]{0,2,1:T(8,128)(2,1)}), bf16[128,16,128]{0,2,1:T(8,128)(2,1)}, u32[]{:S(2)}, u32[]{:S(2)}) async-start(bf16[128,16,128]{0,2,1:T(8,128)(2,1)} %bitcast.197), calls=%async_computation.3 | async-start | bytes 1048576 | tf_op jit(solution)/shard_map/all_to_all | solution.py:54
  155.0 3.9 copy-start.7
  155.0 3.9 copy-start.13
  155.0 3.9 copy-start.17
  159.0 1.6 copy-start.4
  159.8 0.8 copy-start.8
  166.7 4.2 copy-start.7
  166.7 4.2 copy-start.13
  166.7 4.2 copy-start.17
  170.9 1.6 copy-start.4
  171.8 0.8 copy-start.8
  178.7 4.2 copy-start.7
  178.7 4.2 copy-start.13
  178.7 4.2 copy-start.17
  182.9 1.6 copy-start.4
  183.8 0.8 copy-start.8
  190.6 4.2 copy-start.7
  190.6 4.2 copy-start.13
  190.6 4.2 copy-start.17
  194.9 1.6 copy-start.4
  195.7 0.8 copy-start.8
  199.5 18.4 %copy-start.9 = (bf16[2048,1,128]{2,0,1:T(8,128)(2,1)S(1)}, bf16[2048,1,128]{2,0,1:T(8,128)(2,1)}, u32[]{:S(2)}) copy-start(bf16[2048,1,128]{2,0,1:T(8,128)(2,1)} %get-tuple-element.192) | copy-start | bytes 1572868
  205.3 35.5 %all-to-all-start.7 = ((bf16[16,2,8192]{2,1,0:T(2,128)(2,1)}), bf16[16,2,8192]{2,1,0:T(2,128)(2,1)S(1)}, u32[]{:S(2)}, u32[]{:S(2)}) async-start(bf16[16,2,8192]{2,1,0:T(2,128)(2,1)} %reshape.220), calls=%async_computation.7 | async-start | bytes 1048576 | tf_op jit(solution)/shard_map/all_to_all | solution.py:80
  219.6 127.4 %copy-start.16 = (f32[128]{0:T(128)S(1)}, f32[128]{0:T(128)}, u32[]{:S(2)}) copy-start(f32[128]{0:T(128)} %param.13) | copy-start | bytes 1540
  240.8 12.7 %copy-start.5 = (bf16[16,2,8192]{2,1,0:T(2,128)(2,1)}, bf16[16,2,8192]{2,1,0:T(2,128)(2,1)S(1)}, u32[]{:S(2)}) copy-start(bf16[16,2,8192]{2,1,0:T(2,128)(2,1)S(1)} %all-to-all-done.7) | copy-start | bytes 1572868
  240.8 35.6 %all-to-all-start.4 = ((bf16[16,2,8192]{2,1,0:T(2,128)(2,1)}), bf16[16,2,8192]{2,1,0:T(2,128)(2,1)}, u32[]{:S(2)}, u32[]{:S(2)}) async-start(bf16[16,2,8192]{2,1,0:T(2,128)(2,1)} %reshape.218), calls=%async_computation.4 | async-start | bytes 1048576 | tf_op jit(solution)/shard_map/all_to_all | solution.py:79
  334.3 58.0 %all-to-all-start.5 = ((f32[2048,1,128]{2,1,0:T(1,128)}), f32[2048,1,128]{2,1,0:T(1,128)}, u32[]{:S(2)}, u32[]{:S(2)}) async-start(f32[2048,1,128]{2,1,0:T(1,128)} %bitcast.20), calls=%async_computation.5 | async-start | bytes 2097152 | tf_op jit(solution)/shard_map/all_to_all | solution.py:83
  349.7 8.0 %copy-start.1 = (f32[128,16,128]{0,2,1:T(8,128)S(1)}, f32[128,16,128]{0,2,1:T(8,128)}, u32[]{:S(2)}) copy-start(f32[128,16,128]{0,2,1:T(8,128)} %copy-done) | copy-start | bytes 3145732
where the time goes:
time: 511 us; the launch traced here: 509 us
  blocking collectives  168 us (33%)
  waiting for transfers between devices  157 us (31%)
  starting transfers between devices  91.8 us (18%)
  matrix products  43.2 us (8%)
  local copies, waits for them, and re-layouts  35.4 us (7%)
  other arithmetic  13.3 us (3%)
    psum x1, blocking collectives, per_device(): lax.psum(partial_sums, ('grp', 'tp')) * (1.0 / math.sqrt(count_all))  110 us
    all_to_all x1, blocking collectives, per_device(): lax.all_to_all(dk_all, 'tp', split_axis=0, concat_axis=1, tiled=True)  57.9 us
    all_to_all x1, waiting for transfers between devices, per_device(): lax.all_to_all(dq_all, 'tp', split_axis=0, concat_axis=1, tiled=True)  34.2 us
    all_to_all x1, waiting for transfers between devices, per_device(): lax.all_to_all(out_all.astype(jnp.bfloat16), 'tp', split_axis=0, concat_a...  22.2 us
    all_to_all x1, waiting for transfers between devices, per_device(): lax.all_to_all(k_norm, 'tp', split_axis=1, concat_axis=0, tiled=True)  21.8 us
    all_to_all x1, waiting for transfers between devices, per_device(): lax.all_to_all(value3, 'tp', split_axis=1, concat_axis=0, tiled=True)  20.7 us
    all_to_all x1, waiting for transfers between devices, per_device(): lax.all_to_all(q_norm, 'tp', split_axis=1, concat_axis=0, tiled=True)  20.4 us
    unnamed x41, local copies, waits for them, and re-layouts  19.3 us
  transfers between devices with their start and end apart: 7, of which 7 were waited for; matrix products, arithmetic and copies ran while one was open for 5% of the time, Pallas kernels for 0%

commit v1 on v0

v1 whole, which is shorter than its diff:
```python
import functools
import math

import jax
import jax.numpy as jnp
from jax import lax
from jax.experimental import pallas as pl
from jax.experimental.pallas import tpu as pltpu
from jax.sharding import PartitionSpec as P

HD = 128
ROWS = 128
BLK = 16
CAP = 36
PAD = 512
UNROLL = 4
VMEM_BYTES = 40 * 1024 * 1024
F32 = jnp.float32
BF16 = jnp.bfloat16


def boundary(left_row, right_row):
    a = jnp.sum(jnp.where(left_row == right_row[:, :1], 1.0, 0.0)).astype(jnp.int32)
    b = jnp.sum(jnp.where(right_row == left_row[:, ROWS - 1 :], 1.0, 0.0)).astype(jnp.int32)
    return a, b


def plan(a, b, exists, heads):
    crosses = jnp.where(jnp.logical_and(exists, a > 0), 1, 0).astype(jnp.int32)
    a, b = a * crosses, b * crosses
    na, nb = (a + BLK - 1) // BLK, (b + BLK - 1) // BLK
    both = jnp.maximum(na + nb, 1)
    h = (heads * nb + both // 2) // both
    return a, b, na, nb, h * crosses, (heads - h) * crosses


def write_plan(prm_ref, seg_ref, heads):
    me = lax.axis_index("tp")
    last = seg_ref.shape[0] - 1
    own = seg_ref[pl.ds(me, 1), :]
    prev = seg_ref[pl.ds(jnp.maximum(me - 1, 0), 1), :]
    after = seg_ref[pl.ds(jnp.minimum(me + 1, last), 1), :]
    left = plan(*boundary(prev, own), me > 0, heads)
    right = plan(*boundary(own, after), me < last, heads)
    for i, value in enumerate(left + right):
        prm_ref[i] = value
    return left, right


def head_cols(j):
    return pl.ds(pl.multiple_of(j * HD, HD), HD)


def pack_kernel(heads, q_ref, k_ref, v_ref, g_ref, seg_ref, to_prev, to_next, prm_ref):
    left, right = write_plan(prm_ref, seg_ref, heads)
    refs = (q_ref, k_ref, v_ref, g_ref)

    def send(out_ref, count, first_head, first_row, blocks):
        def head(jj, _):
            cols = head_cols(first_head + jj)

            def rows(r, _):
                src = pl.ds(pl.multiple_of(first_row + r * BLK, BLK), BLK)
                dst = pl.ds(pl.multiple_of((jj * blocks + r) * BLK, BLK), BLK)
                for t, ref in enumerate(refs):
                    out_ref[dst, t * HD : (t + 1) * HD] = ref[src, cols]
                return 0

            return lax.fori_loop(0, blocks, rows, 0)

        lax.fori_loop(0, count, head, 0)

    _, _, _, nb, h, rest = left
    send(to_prev, rest, h, 0, nb)
    _, _, na, _, h, _ = right
    send(to_next, h, 0, ROWS - na * BLK, na)


def mm(x, y, dims):
    return lax.dot_general(x, y, (dims, ((), ())), preferred_element_type=F32)


NT = ((1,), (1,))
NN = ((1,), (0,))
TN = ((0,), (0,))


def unit_attention(q, k, v, g, mask, row_ok, q_gain, k_gain, scale):
    def normed(x, gain):
        xf = x.astype(F32)
        recip = lax.rsqrt(jnp.sum(xf * xf, axis=-1, keepdims=True) * (1.0 / HD) + 1e-06)
        unit = xf * recip
        return unit, recip, (unit * gain).astype(BF16)

    def back(unit, recip, grad, gain):
        scaled = grad * (gain * scale)
        inner = jnp.sum(scaled * unit, axis=-1, keepdims=True) * (1.0 / HD)
        return (recip * (scaled - unit * inner)).astype(BF16)

    q_unit, q_recip, q_norm = normed(q, q_gain)
    k_unit, k_recip, k_norm = normed(k, k_gain)
    scores = mm(q_norm, k_norm, NT)
    weight = jnp.where(mask, jnp.exp2(scores * (scale * math.log2(math.e))), 0.0)
    total = jnp.sum(weight, axis=-1, keepdims=True)
    probs = weight * (1.0 / jnp.where(row_ok, total, 1.0))
    rounded = probs.astype(BF16)
    out = mm(rounded, v, NN)
    dprobs = mm(g, v, NT)
    delta = jnp.sum(g.astype(F32) * out, axis=-1, keepdims=True)
    dscores = (probs * (dprobs - delta)).astype(BF16)
    dq = mm(dscores, k_norm, NN)
    dk = mm(dscores, q_norm, TN)
    dv = mm(rounded, g, TN)
    results = (
        out.astype(BF16),
        back(q_unit, q_recip, dq, q_gain),
        back(k_unit, k_recip, dk, k_gain),
        dv.astype(BF16),
    )
    return results, dq * q_unit, dk * k_unit


def fold(x):
    return jnp.sum(x.reshape(ROWS // 8, 8, HD), axis=0)


def row_ids():
    return lax.broadcasted_iota(jnp.int32, (ROWS, 1), 0)


def local_kernel(heads, scale, prm_ref, q_ref, k_ref, v_ref, g_ref, seg_ref, qg_ref, kg_ref, o_ref, dq_ref, dk_ref, dv_ref, sums_ref):
    me = lax.axis_index("tp")
    own = jnp.broadcast_to(seg_ref[pl.ds(me, 1), :].astype(F32), (ROWS, ROWS))
    same = own == own.T
    rows = row_ids()
    whole = jnp.logical_and(rows >= prm_ref[1], rows < ROWS - prm_ref[6])
    q_gain, k_gain = qg_ref[...], kg_ref[...]
    sums_ref[...] = jnp.zeros_like(sums_ref)

    def group(i, _):
        for u in range(UNROLL):
            cols = head_cols(i * UNROLL + u)
            results, gq, gk = unit_attention(
                q_ref[:, cols], k_ref[:, cols], v_ref[:, cols], g_ref[:, cols], same, rows >= 0, q_gain, k_gain, scale
            )
            for ref, value in zip((o_ref, dq_ref, dk_ref, dv_ref), results):
                ref[:, cols] = value
            sums_ref[0:8, :] += fold(jnp.where(whole, gq, 0.0))
            sums_ref[8:16, :] += fold(jnp.where(whole, gk, 0.0))
        return 0

    lax.fori_loop(0, heads // UNROLL, group, 0)


def cross_kernel(heads, scale, prm_ref, q_ref, k_ref, v_ref, g_ref, from_prev, from_next, qg_ref, kg_ref, part_ref,
                 o_ref, dq_ref, dk_ref, dv_ref, to_prev, to_next, gains_ref, in_l, in_r, out_l, out_r, sums):
    size = CAP * BLK
    in_l[PAD : PAD + size, :] = from_prev[...]
    in_r[PAD : PAD + size, :] = from_next[...]
    rows = row_ids()
    cols_id = lax.broadcasted_iota(jnp.int32, (1, ROWS), 1)
    q_gain, k_gain = qg_ref[...], kg_ref[...]
    own_refs = (q_ref, k_ref, v_ref, g_ref)
    res_refs = (o_ref, dq_ref, dk_ref, dv_ref)
    sums[...] = part_ref[...]

    def one(j, a, b, start, in_pad, out_pad, prev_side):
        cols = head_cols(j)
        tail, tail_c = rows >= ROWS - a, cols_id >= ROWS - a
        lead, lead_c = rows < b, cols_id < b
        ok, ok_c = jnp.logical_or(tail, lead), jnp.logical_or(tail_c, lead_c)
        theirs, mine = (tail, lead) if prev_side else (lead, tail)
        window = pl.ds(pl.multiple_of(start, BLK), ROWS)
        merged = [
            jnp.where(theirs, in_pad[window, t * HD : (t + 1) * HD], ref[:, cols]) for t, ref in enumerate(own_refs)
        ]
        results, gq, gk = unit_attention(*merged, jnp.logical_and(ok, ok_c), ok, q_gain, k_gain, scale)
        for t, (ref, value) in enumerate(zip(res_refs, results)):
            ref[:, cols] = jnp.where(mine, value, ref[:, cols])
            out_pad[window, t * HD : (t + 1) * HD] = value
        sums[0:8, :] += fold(gq)
        sums[8:16, :] += fold(gk)

    a, b, na, nb, h, _ = [prm_ref[i] for i in range(6)]
    groups_l = (h + UNROLL - 1) // UNROLL

    def left_group(i, _):
        for u in reversed(range(UNROLL)):
            j = (groups_l - 1 - i) * UNROLL + u
            owned = jnp.where(j < h, 1, 0)
            one(j, a * owned, b * owned, PAD + (j + 1) * na * BLK - ROWS, in_l, out_l, True)
        return 0

    lax.fori_loop(0, groups_l, left_group, 0)

    a2, b2, na2, nb2, h2, rest2 = [prm_ref[6 + i] for i in range(6)]
    first = h2 // UNROLL
    last = jnp.where(rest2 > 0, heads // UNROLL, first)

    def right_group(i, _):
        for u in range(UNROLL):
            j = i * UNROLL + u
            owned = jnp.where(j >= h2, 1, 0)
            one(j, a2 * owned, b2 * owned, PAD + (j - h2) * nb2 * BLK, in_r, out_r, False)
        return 0

    lax.fori_loop(first, last, right_group, 0)
    to_prev[...] = out_l[PAD : PAD + size, :]
    to_next[...] = out_r[PAD : PAD + size, :]
    both = jnp.concatenate(
        [jnp.sum(sums[0:8, :], axis=0, keepdims=True), jnp.sum(sums[8:16, :], axis=0, keepdims=True)], axis=0
    )
    gains_ref[...] = jnp.broadcast_to((both * scale)[None], gains_ref.shape)


def merge_kernel(heads, prm_ref, from_prev, from_next, *refs):
    local, cross, final, (in_l, in_r) = refs[0:4], refs[4:8], refs[8:12], refs[12:14]
    size = CAP * BLK
    in_l[PAD : PAD + size, :] = from_prev[...]
    in_r[PAD : PAD + size, :] = from_next[...]
    rows = row_ids()
    _, b, _, nb, h, _ = [prm_ref[i] for i in range(6)]
    a2, _, na2, _, h2, _ = [prm_ref[6 + i] for i in range(6)]
    lead, tail = rows < b, rows >= ROWS - a2

    def group(i, _):
        for u in range(UNROLL):
            j = i * UNROLL + u
            cols = head_cols(j)
            lead_own = rows < b * jnp.where(j < h, 1, 0)
            tail_own = rows >= ROWS - a2 * jnp.where(j >= h2, 1, 0)
            win_l = pl.ds(pl.multiple_of(PAD + jnp.maximum(j - h, 0) * nb * BLK, BLK), ROWS)
            win_r = pl.ds(pl.multiple_of(PAD + (jnp.minimum(j, h2) + 1) * na2 * BLK - ROWS, BLK), ROWS)
            for t in range(4):
                lanes = slice(t * HD, (t + 1) * HD)
                value = jnp.where(lead, in_l[win_l, lanes], local[t][:, cols])
                value = jnp.where(tail, in_r[win_r, lanes], value)
                final[t][:, cols] = jnp.where(jnp.logical_or(lead_own, tail_own), cross[t][:, cols], value)
        return 0

    lax.fori_loop(0, heads // UNROLL, group, 0)


VM = pl.BlockSpec(memory_space=pltpu.VMEM)
SM = pl.BlockSpec(memory_space=pltpu.SMEM)


def call(body, in_specs, out_specs, out_shape, flops, scratch=()):
    return pl.pallas_call(
        body,
        in_specs=in_specs,
        out_specs=out_specs,
        out_shape=out_shape,
        scratch_shapes=list(scratch),
        compiler_params=pltpu.CompilerParams(vmem_limit_bytes=VMEM_BYTES),
        cost_estimate=pl.CostEstimate(flops=flops, bytes_accessed=1 << 22, transcendentals=0),
    )


def per_device(queries, keys, values, upstream, q_gain, k_gain, segments):
    rows, width = queries.shape[1:]
    heads = width // HD
    scale = 1.0 / math.sqrt(HD)
    groups, ring = lax.axis_size("grp"), lax.axis_size("tp")
    args = (queries[0], keys[0], values[0], upstream[0])
    seg = segments[0].reshape(ring, rows)
    gains = (q_gain.reshape(1, HD), k_gain.reshape(1, HD))
    full = jax.ShapeDtypeStruct((rows, width), BF16)
    sent = jax.ShapeDtypeStruct((CAP * BLK, 4 * HD), BF16)
    pad = pltpu.VMEM((CAP * BLK + 2 * PAD, 4 * HD), BF16)
    up = [(i, i + 1) for i in range(ring - 1)]
    down = [(i + 1, i) for i in range(ring - 1)]

    to_prev, to_next, prm = call(
        functools.partial(pack_kernel, heads),
        [VM] * 5,
        [VM, VM, SM],
        [sent, sent, jax.ShapeDtypeStruct((12,), jnp.int32)],
        1 << 20,
    )(*args, seg)
    from_prev = lax.ppermute(to_next, "tp", up)
    from_next = lax.ppermute(to_prev, "tp", down)
    *local, part = call(
        functools.partial(local_kernel, heads, scale),
        [SM] + [VM] * 7,
        [VM] * 5,
        [full] * 4 + [jax.ShapeDtypeStruct((16, HD), F32)],
        1 << 30,
    )(prm, *args, seg, *gains)
    *cross, back_prev, back_next, sums = call(
        functools.partial(cross_kernel, heads, scale),
        [SM] + [VM] * 9,
        [VM] * 7,
        [full] * 4 + [sent, sent, jax.ShapeDtypeStruct((groups, 2, HD), F32)],
        1 << 30,
        [pad] * 4 + [pltpu.VMEM((16, HD), F32)],
    )(prm, *args, from_prev, from_next, *gains, part)
    done_next = lax.ppermute(back_prev, "tp", down)
    done_prev = lax.ppermute(back_next, "tp", up)
    sums = jnp.sum(lax.all_to_all(sums, "grp", 0, 0), axis=0)
    sums = jnp.sum(lax.all_to_all(jnp.broadcast_to(sums, (ring, 2, HD)), "tp", 0, 0), axis=0)
    gain_grads = sums * (1.0 / math.sqrt(groups * ring * rows * heads))
    outs = call(
        functools.partial(merge_kernel, heads),
        [SM] + [VM] * 10,
        [VM] * 4,
        [full] * 4,
        1 << 20,
        [pad] * 2,
    )(prm, done_prev, done_next, *local, *cross)
    return tuple(x[None] for x in outs) + (gain_grads,)


def solution(mesh):
    row = P("grp", "tp", None)
    in_specs = (row, row, row, row, P(), P(), P("grp", None))
    out_specs = (row, row, row, row, P())
    return jax.shard_map(per_device, mesh=mesh, in_specs=in_specs, out_specs=out_specs, check_vma=False)
```

time: 511 us -> 105 us (0.21)
  waiting for transfers between devices: 157 us -> 0.98 us
  blocking collectives: 168 us -> 51.8 us
  starting transfers between devices: 91.8 us -> 13 us
  matrix products: 43.2 us -> 0 us
  Pallas kernels: 0 us -> 24.5 us
  local copies, waits for them, and re-layouts: 35.4 us -> 12.9 us
  other arithmetic: 13.3 us -> 0.64 us
    all_to_all x7 -> x0, waiting for transfers between devices: 157 us -> none  [the longest x1 34.2 us: per_device(): lax.all_to_all(dq_all, 'tp', split_axis=0, concat_axis=1, tiled=True)]
    psum x1 -> x0, blocking collectives: 110 us -> none  [per_device(): lax.psum(partial_sums, ('grp', 'tp')) * (1.0 / math.sqrt(count_all))]
    all_to_all x7 -> x0, starting transfers between devices: 91.8 us -> none  [the longest x1 15.7 us: per_device(): lax.all_to_all(q_norm, 'tp', split_axis=1, concat_axis=0, tiled=True)]
    dot_general x24 -> x0, matrix products: 43.2 us -> none  [the longest x4 16.6 us: attend(): jnp.einsum('hqk,qhd->khd', rounded, grad_h, preferred_element_type=jnp.fl...]
    pallas_call x0 -> x4, Pallas kernels: none -> 24.5 us  [the longest x1 10.3 us: per_device(): call(functools.partial(local_kernel, heads, scale), [SM] + [VM] * 7, [VM]...]
    ppermute x0 -> x4, starting transfers between devices: none -> 13 us  [the longest x1 5.65 us: per_device(): done_prev = lax.ppermute(back_next, 'tp', up)]
    all_to_all x8 -> x0, local copies, waits for them, and re-layouts: 10.4 us -> none  [the longest x1 2.04 us: per_device(): lax.all_to_all(value3, 'tp', split_axis=1, concat_axis=0, tiled=True)]
    convert_element_type x7 -> x0, other arithmetic: 10.3 us -> none  [the longest x2 3 us: per_device(): dv_all.astype(jnp.bfloat16)]
  transfers between devices with their start and end apart: 7 -> 4, of which waited for: 7 -> 1; matrix products, arithmetic and copies ran while one was open for 5% -> 1% of each run, Pallas kernels for 0% -> 10%
where the time goes in v1:
time: 105 us; the launch traced here: 104 us
  blocking collectives  51.8 us (49%)
  Pallas kernels  24.5 us (23%)
  starting transfers between devices  13 us (12%)
  local copies, waits for them, and re-layouts  12.9 us (12%)
    all_to_all x1, blocking collectives, per_device(): lax.all_to_all(jnp.broadcast_to(sums, (ring, 2, HD)), 'tp', 0, 0)  29.1 us
    all_to_all x1, blocking collectives, per_device(): sums = jnp.sum(lax.all_to_all(sums, 'grp', 0, 0), axis=0)  22.7 us
    unnamed x30, local copies, waits for them, and re-layouts  12.8 us
    pallas_call x1, Pallas kernels, per_device(): call(functools.partial(local_kernel, heads, scale), [SM] + [VM] * 7, [VM]...  10.3 us
    pallas_call x1, Pallas kernels, per_device(): call(functools.partial(cross_kernel, heads, scale), [SM] + [VM] * 9, [VM]...  9.28 us
    ppermute x1, starting transfers between devices, per_device(): done_prev = lax.ppermute(back_next, 'tp', up)  5.65 us
    ppermute x1, starting transfers between devices, per_device(): from_prev = lax.ppermute(to_next, 'tp', up)  4.72 us
    pallas_call x1, Pallas kernels, per_device(): call(functools.partial(merge_kernel, heads), [SM] + [VM] * 10, [VM] * 4,...  3.65 us
  transfers between devices with their start and end apart: 4, of which 1 were waited for; matrix products, arithmetic and copies ran while one was open for 1% of the time, Pallas kernels for 10%

profile of v1, /device:TPU:1, one launch (start us, length us, event | category | flops | bytes accessed | tf_op | source)
XLA Modules:
  0.0 104.5 jit_solution(15157234304964681563)
XLA Ops:
  0.6 0.0 copy-start.12
  0.6 0.7 copy-done.12
  1.3 0.0 copy-start
  1.3 1.0 copy-done
  2.4 0.0 copy-start.1
  2.4 1.0 copy-done.1
  3.4 0.0 copy-start.2
  3.4 1.0 copy-done.2
  4.5 0.0 copy-start.3
  4.5 1.0 copy-done.3
  5.5 1.2 %shard_map.110 = (bf16[576,512]{1,0:T(8,128)(2,1)S(1)}, bf16[576,512]{1,0:T(8,128)(2,1)S(1)}, s32[12]{0:T(128)S(1)}) custom-call(bf16[128,2048]{1,0:T(8,128)(2,1)S(1)} %bitcast.11, bf16[128,2048]{1,0:T(8,128)(2,1)S(1)} %bitcast.14, bf16[128,2048]{1,0:T(8,128)(2,1)S(1)} %bitcast.17, bf16[128,2048]{1,0:T(8,128)(2,1)S(1)} %bitcast.20, s32[16,128]{1,0:T(8,128)S(1)} %bitcast.23), custom_call_target="tpu_custom_call" | custom-call | flops 1048576 | bytes 4194304 | tf_op jit(solution)/shard_map/pallas_call | solution.py:274
  6.7 4.7 %collective-permute-start = (bf16[576,512]{1,0:T(8,128)(2,1)S(1)}, bf16[576,512]{1,0:T(8,128)(2,1)S(1)}, u32[]{:S(2)}, u32[]{:S(2)}) collective-permute-start(bf16[576,512]{1,0:T(8,128)(2,1)S(1)} %get-tuple-element.25), channel_id=1, source_target_pairs={{0,1},{1,2},{2,3},{3,4},{4,5},{5,6},{6,7},{7,8},{8,9},{9,10},{10,1... | collective-permute-start | bytes 1769480 | tf_op jit(solution)/shard_map/ppermute | solution.py:281
  11.5 1.3 %collective-permute-start.1 = (bf16[576,512]{1,0:T(8,128)(2,1)S(1)}, bf16[576,512]{1,0:T(8,128)(2,1)S(1)}, u32[]{:S(2)}, u32[]{:S(2)}) collective-permute-start(bf16[576,512]{1,0:T(8,128)(2,1)S(1)} %get-tuple-element.26), channel_id=1, source_target_pairs={{1,0},{2,1},{3,2},{4,3},{5,4},{6,5},{7,6},{8,7},{9,8},{10,9},{11,1... | collective-permute-start | bytes 1769480 | tf_op jit(solution)/shard_map/ppermute | solution.py:282
  12.8 0.0 copy-start.13
  12.8 0.0 copy-start.14
  12.8 0.6 copy-done.13
  13.4 0.0 copy-done.14
  13.4 10.3 %shard_map.111 = (bf16[128,2048]{1,0:T(8,128)(2,1)S(1)}, bf16[128,2048]{1,0:T(8,128)(2,1)S(1)}, bf16[128,2048]{1,0:T(8,128)(2,1)S(1)}, bf16[128,2048]{1,0:T(8,128)(2,1)S(1)}, f32[16,128]{1,0:T(8,128)S(1)}) custom-call(s32[12]{0:T(128)S(1)} %get-tuple-element.24.prm_ref, bf16[128,2048]{1,0:T(8,128)(2,1)S(1)} %bitcast.12, bf16[128,2048]{1,0:T(8,128)(2,1)S(1)} %bitcast.15, ...), custom_call_target="tpu_custom_call" | custom-call | flops 1073741824 | bytes 4194304 | tf_op jit(solution)/shard_map/pallas_call | solution.py:283
  23.8 0.0 collective-permute-done.from_prev
  23.8 1.0 collective-permute-done.1.from_next
  24.8 9.3 %shard_map.112 = (bf16[128,2048]{1,0:T(8,128)(2,1)S(1)}, bf16[128,2048]{1,0:T(8,128)(2,1)S(1)}, bf16[128,2048]{1,0:T(8,128)(2,1)S(1)}, bf16[128,2048]{1,0:T(8,12...) custom-call(s32[12]{0:T(128)S(1)} %get-tuple-element.24.prm_ref, ...), custom_call_target="tpu_custom_call" | custom-call | flops 1073741824 | bytes 4194304 | tf_op jit(solution)/shard_map/pallas_call | solution.py:290
  34.1 0.0 copy-start.4
  34.1 0.8 copy-done.4
  34.8 0.0 copy-start.6
  34.8 0.8 copy-done.6
  35.6 0.0 copy-start.8
  35.6 0.8 copy-done.8
  36.4 0.0 copy-start.10
  36.4 0.8 copy-done.10
  37.2 5.7 %collective-permute-start.2 = (bf16[576,512]{1,0:T(8,128)(2,1)}, bf16[576,512]{1,0:T(8,128)(2,1)S(1)}, u32[]{:S(2)}, u32[]{:S(2)}) collective-permute-start(bf16[576,512]{1,0:T(8,128)(2,1)} %get-tuple-element.28), channel_id=1, source_target_pairs={{0,1},{1,2},{2,3},{3,4},{4,5},{5,6},{6,7},{7,8},{8,9},{9,10},{10,1... | collective-permute-start | bytes 1769480 | tf_op jit(solution)/shard_map/ppermute | solution.py:299
  42.9 1.3 %collective-permute-start.3 = (bf16[576,512]{1,0:T(8,128)(2,1)}, bf16[576,512]{1,0:T(8,128)(2,1)S(1)}, u32[]{:S(2)}, u32[]{:S(2)}) collective-permute-start(bf16[576,512]{1,0:T(8,128)(2,1)} %get-tuple-element.29), channel_id=1, source_target_pairs={{1,0},{2,1},{3,2},{4,3},{5,4},{6,5},{7,6},{8,7},{9,8},{10,9},{11,1... | collective-permute-start | bytes 1769480 | tf_op jit(solution)/shard_map/ppermute | solution.py:298
  44.2 22.7 %all_to_all.10 = f32[32,2,128]{2,1,0:T(2,128)S(1)} all-to-all(f32[32,2,128]{2,1,0:T(2,128)S(1)} %get-tuple-element.42), channel_id=1, replica_groups=mesh['grp'=32,'tp'=16] {'grp'}, dimensions={0} | all-to-all | bytes 65536 | tf_op jit(solution)/shard_map/all_to_all | solution.py:300
  67.0 29.1 %all_to_all.11 = f32[16,2,128]{2,1,0:T(2,128)S(1)} all-to-all(f32[16,2,128]{2,1,0:T(2,128)S(1)} %broadcast_in_dim.19), channel_id=1, replica_groups=mesh['grp'=32,'tp'=16] {'tp'}, dimensions={0} | all-to-all | bytes 32768 | tf_op jit(solution)/shard_map/all_to_all | solution.py:301
  96.1 0.6 broadcast_multiply_fusion
  96.7 0.0 collective-permute-done.2.from_prev
  96.7 0.0 collective-permute-done.3.from_next
  96.7 0.0 copy-start.5
  96.7 1.0 copy-done.5
  97.7 0.0 copy-start.7
  97.7 1.0 copy-done.7
  98.7 0.0 copy-start.9
  98.7 1.0 copy-done.9
  99.8 0.0 copy-start.11
  99.8 1.0 copy-done.11
  100.8 3.6 %shard_map.113 = (bf16[128,2048]{1,0:T(8,128)(2,1)}, bf16[128,2048]{1,0:T(8,128)(2,1)}, bf16[128,2048]{1,0:T(8,128)(2,1)}, bf16[128,2048]{1,0:T(8,128)(2,1)}) custom-call(s32[12]{0:T(128)S(1)} %get-tuple-element.24.prm_ref, bf16[576,512]{1,0:T(8,128)(2,1)S(1)} %collective-permute-done.2.from_prev, bf16[576,512]{1,0:T(8,128)(2,1)S(1)} %collective-permute-done.3.from_next, ...), custom_call_target="tpu_custom_call" | custom-call | flops 1048576 | bytes 4194304 | tf_op jit(solution)/shard_map/pallas_call | solution.py:303
  (3 shorter events, 0.1 us)
Async XLA Ops:
  0.6 0.7 copy-start.12
  1.3 1.0 copy-start
  2.4 1.0 copy-start.1
  3.4 1.0 copy-start.2
  4.5 1.0 copy-start.3
  6.7 17.1 %collective-permute-start = (bf16[576,512]{1,0:T(8,128)(2,1)S(1)}, bf16[576,512]{1,0:T(8,128)(2,1)S(1)}, u32[]{:S(2)}, u32[]{:S(2)}) collective-permute-start(bf16[576,512]{1,0:T(8,128)(2,1)S(1)} %get-tuple-element.25), channel_id=1, source_target_pairs={{0,1},{1,2},{2,3},{3,4},{4,5},{5,6},{6,7},{7,8},{8,9},{9,10},{10,1... | collective-permute-start | bytes 1769480 | tf_op jit(solution)/shard_map/ppermute | solution.py:281
  11.5 13.3 %collective-permute-start.1 = (bf16[576,512]{1,0:T(8,128)(2,1)S(1)}, bf16[576,512]{1,0:T(8,128)(2,1)S(1)}, u32[]{:S(2)}, u32[]{:S(2)}) collective-permute-start(bf16[576,512]{1,0:T(8,128)(2,1)S(1)} %get-tuple-element.26), channel_id=1, source_target_pairs={{1,0},{2,1},{3,2},{4,3},{5,4},{6,5},{7,6},{8,7},{9,8},{10,9},{11,1... | collective-permute-start | bytes 1769480 | tf_op jit(solution)/shard_map/ppermute | solution.py:282
  12.8 0.7 copy-start.13
  12.8 0.7 copy-start.14
  34.1 0.8 copy-start.4
  34.8 0.8 copy-start.6
  35.6 0.8 copy-start.8
  36.4 0.8 copy-start.10
  37.2 59.4 %collective-permute-start.2 = (bf16[576,512]{1,0:T(8,128)(2,1)}, bf16[576,512]{1,0:T(8,128)(2,1)S(1)}, u32[]{:S(2)}, u32[]{:S(2)}) collective-permute-start(bf16[576,512]{1,0:T(8,128)(2,1)} %get-tuple-element.28), channel_id=1, source_target_pairs={{0,1},{1,2},{2,3},{3,4},{4,5},{5,6},{6,7},{7,8},{8,9},{9,10},{10,1... | collective-permute-start | bytes 1769480 | tf_op jit(solution)/shard_map/ppermute | solution.py:299
  42.9 53.8 %collective-permute-start.3 = (bf16[576,512]{1,0:T(8,128)(2,1)}, bf16[576,512]{1,0:T(8,128)(2,1)S(1)}, u32[]{:S(2)}, u32[]{:S(2)}) collective-permute-start(bf16[576,512]{1,0:T(8,128)(2,1)} %get-tuple-element.29), channel_id=1, source_target_pairs={{1,0},{2,1},{3,2},{4,3},{5,4},{6,5},{7,6},{8,7},{9,8},{10,9},{11,1... | collective-permute-start | bytes 1769480 | tf_op jit(solution)/shard_map/ppermute | solution.py:298
  96.7 1.0 copy-start.5
  97.7 1.0 copy-start.7
  98.7 1.0 copy-start.9
  99.8 1.0 copy-start.11

commit v2 on v1

v2 whole, which is shorter than its diff:
```python
import functools
import math

import jax
import jax.numpy as jnp
from jax import lax
from jax.experimental import pallas as pl
from jax.experimental.pallas import tpu as pltpu
from jax.sharding import PartitionSpec as P

HD = 128
ROWS = 128
BLK = 16
BATCH = 8
CAPS = (20, 16)
FIRST, SECOND = CAPS[0] * BLK, CAPS[1] * BLK
MIB = 1024 * 1024
F32 = jnp.float32
BF16 = jnp.bfloat16


def padded(size):
    return ROWS, 2 * ROWS + size, 2 * (ROWS + size), 3 * ROWS + 2 * size


def most(blocks):
    first = jnp.minimum(CAPS[0] // jnp.maximum(blocks, 1), BATCH)
    return first, first + CAPS[1] // jnp.maximum(blocks, 1)


def plan(left_row, right_row, exists, heads):
    a = jnp.sum(jnp.where(left_row == right_row[:, :1], 1.0, 0.0)).astype(jnp.int32)
    b = jnp.sum(jnp.where(right_row == left_row[:, ROWS - 1 :], 1.0, 0.0)).astype(jnp.int32)
    crosses = jnp.where(jnp.logical_and(exists, a > 0), 1, 0).astype(jnp.int32)
    a, b = a * crosses, b * crosses
    na, nb = (a + BLK - 1) // BLK, (b + BLK - 1) // BLK
    first_a, all_a = most(na)
    first_b, all_b = most(nb)
    h = jnp.minimum(jnp.maximum(heads // 2, heads - all_b), all_a)
    rest = (heads - h) * crosses
    h = h * crosses
    return a, b, na, nb, h, rest, jnp.minimum(h, first_a), jnp.minimum(rest, first_b)


def write_plan(prm_ref, seg_ref, heads):
    me = lax.axis_index("tp")
    last = seg_ref.shape[0] - 1
    own = seg_ref[pl.ds(me, 1), :]
    prev = seg_ref[pl.ds(jnp.maximum(me - 1, 0), 1), :]
    after = seg_ref[pl.ds(jnp.minimum(me + 1, last), 1), :]
    left = plan(prev, own, me > 0, heads)
    right = plan(own, after, me < last, heads)
    for i, value in enumerate(left + right):
        prm_ref[i] = value
    return left, right


def head_cols(j):
    return pl.ds(pl.multiple_of(j * HD, HD), HD)


def pack_kernel(heads, q_hbm, k_hbm, v_hbm, g_hbm, seg_hbm, to_prev, to_next, to_prev2, to_next2, prm_ref, q_ref, k_ref, v_ref, g_ref, seg_ref, sem):
    refs = (q_ref, k_ref, v_ref, g_ref)
    step = ROWS // 4
    copies = []
    first = pltpu.make_async_copy(seg_hbm, seg_ref, sem.at[16])
    first.start()
    for t, (src, dst) in enumerate(zip((q_hbm, k_hbm, v_hbm, g_hbm), refs)):
        for r in range(4):
            part = pl.ds(r * step, step)
            copies.append(pltpu.make_async_copy(src.at[part, :], dst.at[part, :], sem.at[t * 4 + r]))
            copies[-1].start()
    first.wait()
    left, right = write_plan(prm_ref, seg_ref, heads)
    for copy in copies:
        copy.wait()

    def send(out_ref, count, first_head, first_row, blocks):
        def head(jj, _):
            cols = head_cols(first_head + jj)

            def rows(r, _):
                src = pl.ds(pl.multiple_of(first_row + r * BLK, BLK), BLK)
                dst = pl.ds(pl.multiple_of((jj * blocks + r) * BLK, BLK), BLK)
                for t, ref in enumerate(refs):
                    out_ref[dst, t * HD : (t + 1) * HD] = ref[src, cols]
                return 0

            return lax.fori_loop(0, blocks, rows, 0)

        lax.fori_loop(0, count, head, 0)

    _, _, _, nb, h, rest, _, one = left
    _, _, na, _, h2, _, one2, _ = right
    send(to_prev, one, h, 0, nb)
    send(to_next, one2, 0, ROWS - na * BLK, na)
    send(to_prev2, rest - one, h + one, 0, nb)
    send(to_next2, h2 - one2, one2, ROWS - na * BLK, na)


def mm(x, y, dims):
    return lax.dot_general(x, y, (dims, ((), ())), preferred_element_type=F32)


NT = ((1,), (1,))
NN = ((1,), (0,))
TN = ((0,), (0,))


def averager():
    r = lax.broadcasted_iota(jnp.int32, (2 * HD, 2 * HD), 0) // HD
    c = lax.broadcasted_iota(jnp.int32, (2 * HD, 2 * HD), 1) // HD
    return jnp.where(r == c, 1.0 / HD, 0.0).astype(BF16)


def units_attention(items, q_gain, k_gain, scale, mean_of):
    n = range(len(items))
    q, k, v, g, mask, row_ok = zip(*items)

    def means(x, y):
        both = [mm(jnp.concatenate([x[i].astype(BF16), y[i].astype(BF16)], axis=1), mean_of, NN) for i in n]
        return [b[:, :HD] for b in both], [b[:, HD:] for b in both]

    qf, kf = [x.astype(F32) for x in q], [x.astype(F32) for x in k]
    q_mean, k_mean = means([x * x for x in qf], [x * x for x in kf])
    q_recip, k_recip = [lax.rsqrt(x + 1e-06) for x in q_mean], [lax.rsqrt(x + 1e-06) for x in k_mean]
    q_unit, k_unit = [qf[i] * q_recip[i] for i in n], [kf[i] * k_recip[i] for i in n]
    q_norm, k_norm = [(x * q_gain).astype(BF16) for x in q_unit], [(x * k_gain).astype(BF16) for x in k_unit]
    scores = [mm(q_norm[i], k_norm[i], NT) for i in n]
    weight = [
        jnp.where(mask[i], jnp.exp2(scores[i] * (scale * math.log2(math.e))), 0.0).astype(BF16) for i in n
    ]
    ones = jnp.ones((ROWS, HD), BF16)
    sums = [mm(weight[i], jnp.concatenate([v[i], ones], axis=1), NN) for i in n]
    total = [x[:, HD:] for x in sums]
    total = [t if ok is None else jnp.where(ok, t, 1.0) for t, ok in zip(total, row_ok)]
    recip = [1.0 / t for t in total]
    out = [sums[i][:, :HD] * recip[i] for i in n]
    g_part = [g[i].astype(F32) * recip[i] for i in n]
    g_both = [jnp.concatenate([g_part[i].astype(BF16), (g_part[i] * out[i]).astype(BF16)], axis=1) for i in n]
    dprobs = [mm(g_both[i], jnp.concatenate([v[i], -ones], axis=1), NT) for i in n]
    dscores = [(weight[i].astype(F32) * dprobs[i]).astype(BF16) for i in n]
    dv = [mm(weight[i], g_both[i][:, :HD], TN) for i in n]
    dq = [mm(dscores[i], k_norm[i], NN) for i in n]
    dk = [mm(dscores[i], q_norm[i], TN) for i in n]
    q_scaled, k_scaled = [x * (q_gain * scale) for x in dq], [x * (k_gain * scale) for x in dk]
    q_part, k_part = [q_scaled[i] * q_unit[i] for i in n], [k_scaled[i] * k_unit[i] for i in n]
    q_inner, k_inner = means(q_part, k_part)
    results = [
        (
            out[i].astype(BF16),
            (q_recip[i] * (q_scaled[i] - q_unit[i] * q_inner[i])).astype(BF16),
            (k_recip[i] * (k_scaled[i] - k_unit[i] * k_inner[i])).astype(BF16),
            dv[i].astype(BF16),
        )
        for i in n
    ]
    return results, q_part, k_part


def fold(x):
    return jnp.sum(x.reshape(ROWS // 8, 8, HD), axis=0)


def row_ids():
    return lax.broadcasted_iota(jnp.int32, (ROWS, 1), 0)


def local_kernel(heads, scale, prm_ref, q_ref, k_ref, v_ref, g_ref, seg_ref, qg_ref, kg_ref, o_ref, dq_ref, dk_ref, dv_ref, sums_ref):
    me = lax.axis_index("tp")
    own = jnp.broadcast_to(seg_ref[pl.ds(me, 1), :].astype(F32), (ROWS, ROWS))
    same = own == own.T
    rows = row_ids()
    whole = jnp.logical_and(rows >= prm_ref[1], rows < ROWS - prm_ref[8])
    q_gain, k_gain = qg_ref[...], kg_ref[...]
    mean_of = averager()
    sums_ref[...] = jnp.zeros_like(sums_ref)

    def group(i, _):
        cols = [head_cols(i * BATCH + u) for u in range(BATCH)]
        items = [(q_ref[:, c], k_ref[:, c], v_ref[:, c], g_ref[:, c], same, None) for c in cols]
        results, gq, gk = units_attention(items, q_gain, k_gain, scale, mean_of)
        for c, res in zip(cols, results):
            for ref, value in zip((o_ref, dq_ref, dk_ref, dv_ref), res):
                ref[:, c] = value
        sums_ref[0:8, :] += fold(jnp.where(whole, sum(gq), 0.0))
        sums_ref[8:16, :] += fold(jnp.where(whole, sum(gk), 0.0))
        return 0

    lax.fori_loop(0, heads // BATCH, group, 0)


def cross_kernel(heads, second, prm_ref, *refs):
    own, (from_prev, from_next, qg_ref, kg_ref, part_ref), local, refs = refs[0:4], refs[4:9], refs[9:13], refs[13:]
    if second:
        (first_prev, first_next), refs = refs[0:2], refs[2:]
    final, (to_prev, to_next, gains_ref, in_pad, out_pad, sums) = refs[0:4], refs[4:]
    size = from_prev.shape[0]
    left, right, spare, _ = padded(size)
    in_pad[left : left + size, :] = from_prev[...]
    in_pad[right : right + size, :] = from_next[...]
    for src, dst in zip(local, final):
        dst[...] = src[...]
    sums[...] = part_ref[...]
    rows = row_ids()
    cols_id = lax.broadcasted_iota(jnp.int32, (1, ROWS), 1)
    q_gain, k_gain = qg_ref[...], kg_ref[...]
    mean_of = averager()
    a_l, b_l, na_l, _, h_l, _, one_l, _ = [prm_ref[i] for i in range(8)]
    a_r, b_r, _, nb_r, h_r, rest_r, _, one_r = [prm_ref[8 + i] for i in range(8)]
    if second:
        base_l, num_l, base_r, num_r = one_l, h_l - one_l, h_r + one_r, rest_r - one_r
    else:
        base_l, num_l, base_r, num_r = 0, one_l, h_r, one_r
    count = num_l + num_r

    def group(i, _):
        items, places = [], []
        for u in range(BATCH):
            s = i * BATCH + u
            is_l, used = s < num_l, s < count
            n = jnp.where(is_l, num_l - 1 - s, jnp.where(used, s - num_l, 0))
            j = n + jnp.where(is_l, base_l, jnp.where(used, base_r, 0))
            start = jnp.where(
                is_l, left + (n + 1) * na_l * BLK - ROWS, jnp.where(used, right + n * nb_r * BLK, spare)
            )
            a = jnp.where(is_l, a_l, jnp.where(used, a_r, 0))
            b = jnp.where(is_l, b_l, jnp.where(used, b_r, 0))
            ok = jnp.logical_or(rows >= ROWS - a, rows < b)
            ok_c = jnp.logical_or(cols_id >= ROWS - a, cols_id < b)
            low = jnp.where(is_l, ROWS - a, 0)
            high = jnp.where(is_l, ROWS, b)
            theirs = jnp.logical_and(rows >= low, rows < high)
            mine = jnp.logical_and(ok, jnp.logical_not(theirs))
            cols = head_cols(j)
            window = pl.ds(pl.multiple_of(start, BLK), ROWS)
            merged = [
                jnp.where(theirs, in_pad[window, t * HD : (t + 1) * HD], ref[:, cols]) for t, ref in enumerate(own)
            ]
            items.append((*merged, jnp.logical_and(ok, ok_c), ok))
            places.append((cols, window, mine))
        results, gq, gk = units_attention(items, q_gain, k_gain, 1.0 / math.sqrt(HD), mean_of)
        for (cols, window, mine), res in zip(places, results):
            for t, (ref, value) in enumerate(zip(final, res)):
                ref[:, cols] = jnp.where(mine, value, ref[:, cols])
                out_pad[window, t * HD : (t + 1) * HD] = value
        sums[0:8, :] += fold(sum(gq))
        sums[8:16, :] += fold(sum(gk))
        return 0

    lax.fori_loop(0, (count + BATCH - 1) // BATCH, group, 0)
    if not second:
        to_prev[...] = out_pad[left : left + size, :]
        to_next[...] = out_pad[right : right + size, :]
        gains_ref[...] = sums[...]
        return
    for out_ref, start, first in ((to_prev, left, first_prev), (to_next, right, first_next)):
        out_ref[:FIRST, :] = first[...]
        out_ref[FIRST:, :] = out_pad[start : start + size, :]
    both = jnp.concatenate(
        [
            jnp.sum(sums[0:8, :], axis=0, keepdims=True) / q_gain,
            jnp.sum(sums[8:16, :], axis=0, keepdims=True) / k_gain,
        ],
        axis=0,
    )
    gains_ref[...] = jnp.broadcast_to(both[None], gains_ref.shape)


def merge_kernel(heads, prm_ref, from_prev, from_next, *refs):
    local, final, pad = refs[0:4], refs[4:8], refs[8]
    step = pl.program_id(0)

    left, right, _, _ = padded(FIRST + SECOND)

    @pl.when(step == 0)
    def _():
        pad[left : left + FIRST + SECOND, :] = from_prev[...]
        pad[right : right + FIRST + SECOND, :] = from_next[...]

    rows = row_ids()
    _, b, _, nb, h, _, _, one = [prm_ref[i] for i in range(8)]
    a, _, na, _, h2, _, one2, _ = [prm_ref[8 + i] for i in range(8)]
    each = local[0].shape[1] // HD
    for u in range(each):
        j = step * each + u
        lead = rows < b * jnp.where(j >= h, 1, 0)
        tail = rows >= ROWS - a * jnp.where(j < h2, 1, 0)
        n, n2 = jnp.maximum(j - h, 0), jnp.minimum(j, jnp.maximum(h2 - 1, 0))
        at = left + jnp.where(n < one, n * nb * BLK, FIRST + (n - one) * nb * BLK)
        at2 = right + jnp.where(n2 < one2, n2 + 1, n2 + 1 - one2) * na * BLK - ROWS + jnp.where(n2 < one2, 0, FIRST)
        win_l, win_r = pl.ds(pl.multiple_of(at, BLK), ROWS), pl.ds(pl.multiple_of(at2, BLK), ROWS)
        cols = slice(u * HD, (u + 1) * HD)
        for t in range(4):
            lanes = slice(t * HD, (t + 1) * HD)
            value = jnp.where(lead, pad[win_l, lanes], local[t][:, cols])
            final[t][:, cols] = jnp.where(tail, pad[win_r, lanes], value)


VM = pl.BlockSpec(memory_space=pltpu.VMEM)
SM = pl.BlockSpec(memory_space=pltpu.SMEM)
HB = pl.BlockSpec(memory_space=pltpu.HBM)


def call(body, in_specs, out_specs, out_shape, flops, scratch=(), grid=(), vmem=40):
    return pl.pallas_call(
        body,
        grid=grid,
        in_specs=in_specs,
        out_specs=out_specs,
        out_shape=out_shape,
        scratch_shapes=list(scratch),
        compiler_params=pltpu.CompilerParams(vmem_limit_bytes=vmem * MIB),
        cost_estimate=pl.CostEstimate(flops=flops, bytes_accessed=1 << 22, transcendentals=0),
    )


def local_call(heads, args):
    rows, width = args[1].shape
    return call(
        functools.partial(local_kernel, heads, 1.0 / math.sqrt(HD)),
        [SM] + [VM] * 7,
        [VM] * 5,
        [jax.ShapeDtypeStruct((rows, width), BF16)] * 4 + [jax.ShapeDtypeStruct((16, HD), F32)],
        1 << 30,
    )(*args)


def per_device(queries, keys, values, upstream, q_gain, k_gain, segments):
    rows, width = queries.shape[1:]
    heads = width // HD
    groups, ring = lax.axis_size("grp"), lax.axis_size("tp")
    args = (queries[0], keys[0], values[0], upstream[0])
    seg = segments[0].reshape(ring, rows)
    gains = (q_gain.reshape(1, HD), k_gain.reshape(1, HD))
    full = jax.ShapeDtypeStruct((rows, width), BF16)
    sent, sent2, back = [jax.ShapeDtypeStruct((n, 4 * HD), BF16) for n in (FIRST, SECOND, FIRST + SECOND)]
    part = jax.ShapeDtypeStruct((16, HD), F32)
    up = [(i, i + 1) for i in range(ring - 1)]
    down = [(i + 1, i) for i in range(ring - 1)]

    def pad(size):
        return pltpu.VMEM((padded(size)[3], 4 * HD), BF16)

    to_prev, to_next, to_prev2, to_next2, prm, *args, seg = call(
        functools.partial(pack_kernel, heads),
        [HB] * 5,
        [VM] * 4 + [SM] + [VM] * 5,
        [sent, sent, sent2, sent2, jax.ShapeDtypeStruct((16,), jnp.int32)]
        + [full] * 4
        + [jax.ShapeDtypeStruct(seg.shape, seg.dtype)],
        1 << 20,
        [pltpu.SemaphoreType.DMA((17,))],
        vmem=12,
    )(*[pltpu.with_memory_space_constraint(x, pltpu.HBM) for x in (*args, seg)])
    from_prev = lax.ppermute(to_next, "tp", up)
    from_next = lax.ppermute(to_prev, "tp", down)
    from_prev2 = lax.ppermute(to_next2, "tp", up)
    from_next2 = lax.ppermute(to_prev2, "tp", down)
    *local, sums = local_call(heads, (prm, *args, seg, *gains))
    *merged, first_prev, first_next, sums = call(
        functools.partial(cross_kernel, heads, False),
        [SM] + [VM] * 13,
        [VM] * 7,
        [full] * 4 + [sent, sent, part],
        1 << 30,
        [pad(FIRST), pad(FIRST), pltpu.VMEM((16, HD), F32)],
    )(prm, *args, from_prev, from_next, *gains, sums, *local)
    *merged, back_prev, back_next, sums = call(
        functools.partial(cross_kernel, heads, True),
        [SM] + [VM] * 15,
        [VM] * 7,
        [full] * 4 + [back, back, jax.ShapeDtypeStruct((groups, 2, HD), F32)],
        1 << 30,
        [pad(SECOND), pad(SECOND), pltpu.VMEM((16, HD), F32)],
    )(prm, *args, from_prev2, from_next2, *gains, sums, *merged, first_prev, first_next)
    done_next = lax.ppermute(back_prev, "tp", down)
    done_prev = lax.ppermute(back_next, "tp", up)
    sums = jnp.sum(lax.all_to_all(sums, "grp", 0, 0), axis=0)
    block = pl.BlockSpec((rows, width // 4), lambda i: (0, i))
    whole = pl.BlockSpec((FIRST + SECOND, 4 * HD), lambda i: (0, 0))
    outs = call(
        functools.partial(merge_kernel, heads),
        [SM, whole, whole] + [block] * 4,
        [block] * 4,
        [full] * 4,
        1 << 20,
        [pad(FIRST + SECOND)],
        (4,),
        16,
    )(prm, done_prev, done_next, *merged)
    sums = jnp.sum(lax.all_to_all(jnp.broadcast_to(sums, (ring, 2, HD)), "tp", 0, 0), axis=0)
    gain_grads = sums * (1.0 / math.sqrt(groups * ring * rows * heads))
    return tuple(x[None] for x in outs) + (gain_grads,)


def solution(mesh):
    row = P("grp", "tp", None)
    in_specs = (row, row, row, row, P(), P(), P("grp", None))
    out_specs = (row, row, row, row, P())
    return jax.shard_map(per_device, mesh=mesh, in_specs=in_specs, out_specs=out_specs, check_vma=False)
```

time: 105 us -> 84.1 us (0.80)
  local copies, waits for them, and re-layouts: 12.9 us -> 0.67 us
  Pallas kernels: 24.5 us -> 16.1 us
  blocking collectives: 51.8 us -> 48.5 us
  starting transfers between devices: 13 us -> 16 us
    unnamed x30 -> x4, local copies, waits for them, and re-layouts: 12.8 us -> 0.66 us
    pallas_call x4 -> x5, Pallas kernels: 24.5 us -> 16.1 us  [the longest x1 3.98 us: per_device(): call(functools.partial(cross_kernel, heads, True), [SM] + [VM] * 15, [VM]...]
    ppermute x0 -> x2, starting transfers between devices: none -> 5.29 us  [the longest x1 4 us: per_device(): from_prev2 = lax.ppermute(to_next2, 'tp', up)]
    all_to_all x1, blocking collectives: 22.7 us -> 18 us  [per_device(): sums = jnp.sum(lax.all_to_all(sums, 'grp', 0, 0), axis=0)]
    ppermute x1, starting transfers between devices: 5.65 us -> 3.23 us  [per_device(): done_prev = lax.ppermute(back_next, 'tp', up)]
    all_to_all x1, blocking collectives: 29.1 us -> 30.5 us  [per_device(): lax.all_to_all(jnp.broadcast_to(sums, (ring, 2, HD)), 'tp', 0, 0)]
    ppermute x0 -> x2, waiting for transfers between devices: none -> 1.12 us  [the longest x1 1.12 us: per_device(): from_next2 = lax.ppermute(to_prev2, 'tp', down)]
  transfers between devices with their start and end apart: 4 -> 6, of which waited for: 1 -> 1; matrix products, arithmetic and copies ran while one was open for 1% -> 1% of each run, Pallas kernels for 10% -> 8%
where the time goes in v2:
time: 84.1 us; the launch traced here: 83.8 us
  blocking collectives  48.5 us (58%)
  Pallas kernels  16.1 us (19%)
  starting transfers between devices  16 us (19%)
  waiting for transfers between devices  1.13 us (1%)
    all_to_all x1, blocking collectives, per_device(): lax.all_to_all(jnp.broadcast_to(sums, (ring, 2, HD)), 'tp', 0, 0)  30.5 us
    all_to_all x1, blocking collectives, per_device(): sums = jnp.sum(lax.all_to_all(sums, 'grp', 0, 0), axis=0)  18 us
    ppermute x1, starting transfers between devices, per_device(): from_prev = lax.ppermute(to_next, 'tp', up)  4.9 us
    ppermute x1, starting transfers between devices, per_device(): from_prev2 = lax.ppermute(to_next2, 'tp', up)  4 us
    pallas_call x1, Pallas kernels, per_device(): call(functools.partial(cross_kernel, heads, True), [SM] + [VM] * 15, [VM]...  3.98 us
    pallas_call x1, Pallas kernels, local_call(): call(functools.partial(local_kernel, heads, 1.0 / math.sqrt(HD)), [SM] +...  3.37 us
    ppermute x1, starting transfers between devices, per_device(): done_prev = lax.ppermute(back_next, 'tp', up)  3.23 us
    pallas_call x1, Pallas kernels, per_device(): call(functools.partial(merge_kernel, heads), [SM, whole, whole] + [block]...  3.14 us
  transfers between devices with their start and end apart: 6, of which 1 were waited for; matrix products, arithmetic and copies ran while one was open for 1% of the time, Pallas kernels for 8%

profile of v2, /device:TPU:1, one launch (start us, length us, event | category | flops | bytes accessed | tf_op | source)
XLA Modules:
  0.0 83.8 jit_solution(7312477662997812744)
XLA Ops:
  0.6 2.6 %shard_map.110 = (bf16[320,512]{1,0:T(8,128)(2,1)S(1)}, bf16[320,512]{1,0:T(8,128)(2,1)S(1)}, bf16[256,512]{1,0:T(8,128)(2,1)S(1)}, bf16[256,512]{1,0:T(8,128)(2...) custom-call(bf16[128,2048]{1,0:T(8,128)(2,1)} %bitcast.17, ...), custom_call_target="tpu_custom_call" | custom-call | flops 1048576 | bytes 4194304 | tf_op jit(solution)/shard_map/pallas_call | solution.py:345
  3.2 4.9 %collective-permute-start.2 = (bf16[320,512]{1,0:T(8,128)(2,1)S(1)}, bf16[320,512]{1,0:T(8,128)(2,1)S(1)}, u32[]{:S(2)}, u32[]{:S(2)}) collective-permute-start(bf16[320,512]{1,0:T(8,128)(2,1)S(1)} %get-tuple-element.45), channel_id=1, source_target_pairs={{0,1},{1,2},{2,3},{3,4},{4,5},{5,6},{6,7},{7,8},{8,9},{9,10},{10,1... | collective-permute-start | bytes 983048 | tf_op jit(solution)/shard_map/ppermute | solution.py:356
  8.1 1.3 %collective-permute-start.3 = (bf16[320,512]{1,0:T(8,128)(2,1)S(1)}, bf16[320,512]{1,0:T(8,128)(2,1)S(1)}, u32[]{:S(2)}, u32[]{:S(2)}) collective-permute-start(bf16[320,512]{1,0:T(8,128)(2,1)S(1)} %get-tuple-element.46), channel_id=1, source_target_pairs={{1,0},{2,1},{3,2},{4,3},{5,4},{6,5},{7,6},{8,7},{9,8},{10,9},{11,1... | collective-permute-start | bytes 983048 | tf_op jit(solution)/shard_map/ppermute | solution.py:357
  9.4 4.0 %collective-permute-start = (bf16[256,512]{1,0:T(8,128)(2,1)S(1)}, bf16[256,512]{1,0:T(8,128)(2,1)S(1)}, u32[]{:S(2)}, u32[]{:S(2)}) collective-permute-start(bf16[256,512]{1,0:T(8,128)(2,1)S(1)} %get-tuple-element.43), channel_id=1, source_target_pairs={{0,1},{1,2},{2,3},{3,4},{4,5},{5,6},{6,7},{7,8},{8,9},{9,10},{10,1... | collective-permute-start | bytes 786440 | tf_op jit(solution)/shard_map/ppermute | solution.py:358
  13.4 1.3 %collective-permute-start.1 = (bf16[256,512]{1,0:T(8,128)(2,1)S(1)}, bf16[256,512]{1,0:T(8,128)(2,1)S(1)}, u32[]{:S(2)}, u32[]{:S(2)}) collective-permute-start(bf16[256,512]{1,0:T(8,128)(2,1)S(1)} %get-tuple-element.44), channel_id=1, source_target_pairs={{1,0},{2,1},{3,2},{4,3},{5,4},{6,5},{7,6},{8,7},{9,8},{10,9},{11,1... | collective-permute-start | bytes 786440 | tf_op jit(solution)/shard_map/ppermute | solution.py:359
  14.7 0.0 copy-start
  14.7 0.0 copy-start.1
  14.8 0.6 copy-done
  15.4 0.0 copy-done.1
  15.4 3.4 %shard_map.111 = (bf16[128,2048]{1,0:T(8,128)(2,1)S(1)}, bf16[128,2048]{1,0:T(8,128)(2,1)S(1)}, bf16[128,2048]{1,0:T(8,128)(2,1)S(1)}, bf16[128,2048]{1,0:T(8,128)(2,1)S(1)}, f32[16,128]{1,0:T(8,128)S(1)}) custom-call(s32[16]{0:T(128)S(1)} %get-tuple-element.38.prm_ref, bf16[128,2048]{1,0:T(8,128)(2,1)S(1)} %get-tuple-element.39.q_ref.refs_0_, ...), custom_call_target="tpu_custom_call" | custom-call | flops 1073741824 | bytes 4194304 | tf_op jit(solution)/shard_map/pallas_call | solution.py:320
  18.8 0.0 collective-permute-done.2.refs_4_
  18.8 0.0 collective-permute-done.3.refs_5_
  18.8 3.0 %shard_map.112 = (bf16[128,2048]{1,0:T(8,128)(2,1)S(1)}, bf16[128,2048]{1,0:T(8,128)(2,1)S(1)}, bf16[128,2048]{1,0:T(8,128)(2,1)S(1)}, bf16[128,2048]{1,0:T(8,12...) custom-call(s32[16]{0:T(128)S(1)} %get-tuple-element.38.prm_ref, ...), custom_call_target="tpu_custom_call" | custom-call | flops 1073741824 | bytes 4194304 | tf_op jit(solution)/shard_map/pallas_call | solution.py:361
  21.8 0.0 collective-permute-done.refs_4_
  21.8 1.1 %collective-permute-done.1.refs_5_ = bf16[256,512]{1,0:T(8,128)(2,1)S(1)} collective-permute-done((bf16[256,512]{1,0:T(8,128)(2,1)S(1)}, bf16[256,512]{1,0:T(8,128)(2,1)S(1)}, u32[]{:S(2)}, u32[]{:S(2)}) %collective-permute-start.1) | collective-permute-done | bytes 262176 | tf_op jit(solution)/shard_map/ppermute | solution.py:359
  23.0 4.0 %shard_map.113 = (bf16[128,2048]{1,0:T(8,128)(2,1)S(1)}, bf16[128,2048]{1,0:T(8,128)(2,1)S(1)}, bf16[128,2048]{1,0:T(8,128)(2,1)S(1)}, bf16[128,2048]{1,0:T(8,12...) custom-call(s32[16]{0:T(128)S(1)} %get-tuple-element.38.prm_ref, ...), custom_call_target="tpu_custom_call" | custom-call | flops 1073741824 | bytes 4194304 | tf_op jit(solution)/shard_map/pallas_call | solution.py:369
  26.9 3.2 %collective-permute-start.4 = (bf16[576,512]{1,0:T(8,128)(2,1)}, bf16[576,512]{1,0:T(8,128)(2,1)S(1)}, u32[]{:S(2)}, u32[]{:S(2)}) collective-permute-start(bf16[576,512]{1,0:T(8,128)(2,1)} %get-tuple-element.60), channel_id=1, source_target_pairs={{0,1},{1,2},{2,3},{3,4},{4,5},{5,6},{6,7},{7,8},{8,9},{9,10},{10,1... | collective-permute-start | bytes 1769480 | tf_op jit(solution)/shard_map/ppermute | solution.py:378
  30.2 1.3 %collective-permute-start.5 = (bf16[576,512]{1,0:T(8,128)(2,1)}, bf16[576,512]{1,0:T(8,128)(2,1)S(1)}, u32[]{:S(2)}, u32[]{:S(2)}) collective-permute-start(bf16[576,512]{1,0:T(8,128)(2,1)} %get-tuple-element.61), channel_id=1, source_target_pairs={{1,0},{2,1},{3,2},{4,3},{5,4},{6,5},{7,6},{8,7},{9,8},{10,9},{11,1... | collective-permute-start | bytes 1769480 | tf_op jit(solution)/shard_map/ppermute | solution.py:377
  31.5 18.0 %all_to_all.10 = f32[32,2,128]{2,1,0:T(2,128)S(1)} all-to-all(f32[32,2,128]{2,1,0:T(2,128)S(1)} %get-tuple-element.70), channel_id=1, replica_groups=mesh['grp'=32,'tp'=16] {'grp'}, dimensions={0} | all-to-all | bytes 65536 | tf_op jit(solution)/shard_map/all_to_all | solution.py:379
  49.5 30.5 %all_to_all.11 = f32[16,2,128]{2,1,0:T(2,128)S(1)} all-to-all(f32[16,2,128]{2,1,0:T(2,128)S(1)} %broadcast_in_dim.19), channel_id=1, replica_groups=mesh['grp'=32,'tp'=16] {'tp'}, dimensions={0} | all-to-all | bytes 32768 | tf_op jit(solution)/shard_map/all_to_all | solution.py:392
  80.0 0.6 broadcast_multiply_fusion
  80.6 0.0 collective-permute-done.4.from_prev
  80.6 0.0 collective-permute-done.5.from_next
  80.6 3.1 %shard_map.114 = (bf16[128,2048]{1,0:T(8,128)(2,1)}, bf16[128,2048]{1,0:T(8,128)(2,1)}, bf16[128,2048]{1,0:T(8,128)(2,1)}, bf16[128,2048]{1,0:T(8,128)(2,1)}) custom-call(s32[16]{0:T(128)S(1)} %get-tuple-element.38.prm_ref, bf16[576,512]{1,0:T(8,128)(2,1)S(1)} %collective-permute-done.4.from_prev, bf16[576,512]{1,0:T(8,128)(2,1)S(1)} %collective-permute-done.5.from_next, ...), custom_call_target="tpu_custom_call" | custom-call | flops 1048576 | bytes 4194304 | tf_op jit(solution)/shard_map/pallas_call | solution.py:382
  (3 shorter events, 0.1 us)
Async XLA Ops:
  3.2 15.6 %collective-permute-start.2 = (bf16[320,512]{1,0:T(8,128)(2,1)S(1)}, bf16[320,512]{1,0:T(8,128)(2,1)S(1)}, u32[]{:S(2)}, u32[]{:S(2)}) collective-permute-start(bf16[320,512]{1,0:T(8,128)(2,1)S(1)} %get-tuple-element.45), channel_id=1, source_target_pairs={{0,1},{1,2},{2,3},{3,4},{4,5},{5,6},{6,7},{7,8},{8,9},{9,10},{10,1... | collective-permute-start | bytes 983048 | tf_op jit(solution)/shard_map/ppermute | solution.py:356
  8.1 10.7 %collective-permute-start.3 = (bf16[320,512]{1,0:T(8,128)(2,1)S(1)}, bf16[320,512]{1,0:T(8,128)(2,1)S(1)}, u32[]{:S(2)}, u32[]{:S(2)}) collective-permute-start(bf16[320,512]{1,0:T(8,128)(2,1)S(1)} %get-tuple-element.46), channel_id=1, source_target_pairs={{1,0},{2,1},{3,2},{4,3},{5,4},{6,5},{7,6},{8,7},{9,8},{10,9},{11,1... | collective-permute-start | bytes 983048 | tf_op jit(solution)/shard_map/ppermute | solution.py:357
  9.4 12.4 %collective-permute-start = (bf16[256,512]{1,0:T(8,128)(2,1)S(1)}, bf16[256,512]{1,0:T(8,128)(2,1)S(1)}, u32[]{:S(2)}, u32[]{:S(2)}) collective-permute-start(bf16[256,512]{1,0:T(8,128)(2,1)S(1)} %get-tuple-element.43), channel_id=1, source_target_pairs={{0,1},{1,2},{2,3},{3,4},{4,5},{5,6},{6,7},{7,8},{8,9},{9,10},{10,1... | collective-permute-start | bytes 786440 | tf_op jit(solution)/shard_map/ppermute | solution.py:358
  13.4 9.5 %collective-permute-start.1 = (bf16[256,512]{1,0:T(8,128)(2,1)S(1)}, bf16[256,512]{1,0:T(8,128)(2,1)S(1)}, u32[]{:S(2)}, u32[]{:S(2)}) collective-permute-start(bf16[256,512]{1,0:T(8,128)(2,1)S(1)} %get-tuple-element.44), channel_id=1, source_target_pairs={{1,0},{2,1},{3,2},{4,3},{5,4},{6,5},{7,6},{8,7},{9,8},{10,9},{11,1... | collective-permute-start | bytes 786440 | tf_op jit(solution)/shard_map/ppermute | solution.py:359
  14.7 0.7 copy-start
  14.7 0.7 copy-start.1
  26.9 53.7 %collective-permute-start.4 = (bf16[576,512]{1,0:T(8,128)(2,1)}, bf16[576,512]{1,0:T(8,128)(2,1)S(1)}, u32[]{:S(2)}, u32[]{:S(2)}) collective-permute-start(bf16[576,512]{1,0:T(8,128)(2,1)} %get-tuple-element.60), channel_id=1, source_target_pairs={{0,1},{1,2},{2,3},{3,4},{4,5},{5,6},{6,7},{7,8},{8,9},{9,10},{10,1... | collective-permute-start | bytes 1769480 | tf_op jit(solution)/shard_map/ppermute | solution.py:378
  30.2 50.4 %collective-permute-start.5 = (bf16[576,512]{1,0:T(8,128)(2,1)}, bf16[576,512]{1,0:T(8,128)(2,1)S(1)}, u32[]{:S(2)}, u32[]{:S(2)}) collective-permute-start(bf16[576,512]{1,0:T(8,128)(2,1)} %get-tuple-element.61), channel_id=1, source_target_pairs={{1,0},{2,1},{3,2},{4,3},{5,4},{6,5},{7,6},{8,7},{9,8},{10,9},{11,1... | collective-permute-start | bytes 1769480 | tf_op jit(solution)/shard_map/ppermute | solution.py:377

commit v3 on v2

--- a/solution.py
+++ b/solution.py
@@ -12,20 +12,11 @@
 ROWS = 128
 BLK = 16
 BATCH = 8
-CAPS = (20, 16)
-FIRST, SECOND = CAPS[0] * BLK, CAPS[1] * BLK
+CAP = 36
+SIZE = CAP * BLK
 MIB = 1024 * 1024
 F32 = jnp.float32
 BF16 = jnp.bfloat16
-
-
-def padded(size):
-    return ROWS, 2 * ROWS + size, 2 * (ROWS + size), 3 * ROWS + 2 * size
-
-
-def most(blocks):
-    first = jnp.minimum(CAPS[0] // jnp.maximum(blocks, 1), BATCH)
-    return first, first + CAPS[1] // jnp.maximum(blocks, 1)
 
 
 def plan(left_row, right_row, exists, heads):
@@ -34,12 +25,9 @@
     crosses = jnp.where(jnp.logical_and(exists, a > 0), 1, 0).astype(jnp.int32)
     a, b = a * crosses, b * crosses
     na, nb = (a + BLK - 1) // BLK, (b + BLK - 1) // BLK
-    first_a, all_a = most(na)
-    first_b, all_b = most(nb)
-    h = jnp.minimum(jnp.maximum(heads // 2, heads - all_b), all_a)
-    rest = (heads - h) * crosses
-    h = h * crosses
-    return a, b, na, nb, h, rest, jnp.minimum(h, first_a), jnp.minimum(rest, first_b)
+    h = jnp.maximum(heads // 2, heads - CAP // jnp.maximum(nb, 1))
+    h = jnp.minimum(h, CAP // jnp.maximum(na, 1))
+    return a, b, na, nb, h * crosses, (heads - h) * crosses
 
 
 def write_plan(prm_ref, seg_ref, heads):
@@ -50,16 +38,22 @@
     after = seg_ref[pl.ds(jnp.minimum(me + 1, last), 1), :]
     left = plan(prev, own, me > 0, heads)
     right = plan(own, after, me < last, heads)
-    for i, value in enumerate(left + right):
-        prm_ref[i] = value
-    return left, right
+    both = []
+    for x in range(2):
+        is_left = lax.rem(me + x, 2)
+        both.append([is_left] + [jnp.where(is_left == 1, p, q) for p, q in zip(left, right)])
+        for i, value in enumerate(both[x]):
+            prm_ref[8 * x + i] = value
+    prm_ref[7] = left[1]
+    prm_ref[15] = right[0]
+    return both
 
 
 def head_cols(j):
     return pl.ds(pl.multiple_of(j * HD, HD), HD)
 
 
-def pack_kernel(heads, q_hbm, k_hbm, v_hbm, g_hbm, seg_hbm, to_prev, to_next, to_prev2, to_next2, prm_ref, q_ref, k_ref, v_ref, g_ref, seg_ref, sem):
+def pack_kernel(heads, q_hbm, k_hbm, v_hbm, g_hbm, seg_hbm, out_ref, out_ref2, prm_ref, q_ref, k_ref, v_ref, g_ref, seg_ref, sem):
     refs = (q_ref, k_ref, v_ref, g_ref)
     step = ROWS // 4
     copies = []
@@ -71,11 +65,16 @@
             copies.append(pltpu.make_async_copy(src.at[part, :], dst.at[part, :], sem.at[t * 4 + r]))
             copies[-1].start()
     first.wait()
-    left, right = write_plan(prm_ref, seg_ref, heads)
+    plans = write_plan(prm_ref, seg_ref, heads)
     for copy in copies:
         copy.wait()
 
-    def send(out_ref, count, first_head, first_row, blocks):
+    for out, (is_left, _, _, na, nb, h, rest) in zip((out_ref, out_ref2), plans):
+        count = jnp.where(is_left == 1, rest, h)
+        blocks = jnp.where(is_left == 1, nb, na)
+        first_head = jnp.where(is_left == 1, h, 0)
+        first_row = jnp.where(is_left == 1, 0, ROWS - na * BLK)
+
         def head(jj, _):
             cols = head_cols(first_head + jj)
 
@@ -83,19 +82,12 @@
                 src = pl.ds(pl.multiple_of(first_row + r * BLK, BLK), BLK)
                 dst = pl.ds(pl.multiple_of((jj * blocks + r) * BLK, BLK), BLK)
                 for t, ref in enumerate(refs):
-                    out_ref[dst, t * HD : (t + 1) * HD] = ref[src, cols]
+                    out[dst, t * HD : (t + 1) * HD] = ref[src, cols]
                 return 0
 
             return lax.fori_loop(0, blocks, rows, 0)
 
         lax.fori_loop(0, count, head, 0)
-
-    _, _, _, nb, h, rest, _, one = left
-    _, _, na, _, h2, _, one2, _ = right
-    send(to_prev, one, h, 0, nb)
-    send(to_next, one2, 0, ROWS - na * BLK, na)
-    send(to_prev2, rest - one, h + one, 0, nb)
-    send(to_next2, h2 - one2, one2, ROWS - na * BLK, na)
 
 
 def mm(x, y, dims):
@@ -171,7 +163,7 @@
     own = jnp.broadcast_to(seg_ref[pl.ds(me, 1), :].astype(F32), (ROWS, ROWS))
     same = own == own.T
     rows = row_ids()
-    whole = jnp.logical_and(rows >= prm_ref[1], rows < ROWS - prm_ref[8])
+    whole = jnp.logical_and(rows >= prm_ref[7], rows < ROWS - prm_ref[15])
     q_gain, k_gain = qg_ref[...], kg_ref[...]
     mean_of = averager()
     sums_ref[...] = jnp.zeros_like(sums_ref)
@@ -190,15 +182,10 @@
     lax.fori_loop(0, heads // BATCH, group, 0)
 
 
-def cross_kernel(heads, second, prm_ref, *refs):
-    own, (from_prev, from_next, qg_ref, kg_ref, part_ref), local, refs = refs[0:4], refs[4:9], refs[9:13], refs[13:]
-    if second:
-        (first_prev, first_next), refs = refs[0:2], refs[2:]
-    final, (to_prev, to_next, gains_ref, in_pad, out_pad, sums) = refs[0:4], refs[4:]
-    size = from_prev.shape[0]
-    left, right, spare, _ = padded(size)
-    in_pad[left : left + size, :] = from_prev[...]
-    in_pad[right : right + size, :] = from_next[...]
+def cross_kernel(heads, x, prm_ref, *refs):
+    own, (received, qg_ref, kg_ref, part_ref), local = refs[0:4], refs[4:8], refs[8:12]
+    final, (back, gains_ref, in_pad, out_pad, sums) = refs[12:16], refs[16:]
+    in_pad[ROWS : ROWS + SIZE, :] = received[...]
     for src, dst in zip(local, final):
         dst[...] = src[...]
     sums[...] = part_ref[...]
@@ -206,26 +193,20 @@
     cols_id = lax.broadcasted_iota(jnp.int32, (1, ROWS), 1)
     q_gain, k_gain = qg_ref[...], kg_ref[...]
     mean_of = averager()
-    a_l, b_l, na_l, _, h_l, _, one_l, _ = [prm_ref[i] for i in range(8)]
-    a_r, b_r, _, nb_r, h_r, rest_r, _, one_r = [prm_ref[8 + i] for i in range(8)]
-    if second:
-        base_l, num_l, base_r, num_r = one_l, h_l - one_l, h_r + one_r, rest_r - one_r
-    else:
-        base_l, num_l, base_r, num_r = 0, one_l, h_r, one_r
-    count = num_l + num_r
+    is_left, a_all, b_all, na, nb, h, rest = [prm_ref[8 * x + i] for i in range(7)]
+    is_l = is_left == 1
+    count = jnp.where(is_l, h, rest)
 
     def group(i, _):
         items, places = [], []
         for u in range(BATCH):
             s = i * BATCH + u
-            is_l, used = s < num_l, s < count
-            n = jnp.where(is_l, num_l - 1 - s, jnp.where(used, s - num_l, 0))
-            j = n + jnp.where(is_l, base_l, jnp.where(used, base_r, 0))
-            start = jnp.where(
-                is_l, left + (n + 1) * na_l * BLK - ROWS, jnp.where(used, right + n * nb_r * BLK, spare)
-            )
-            a = jnp.where(is_l, a_l, jnp.where(used, a_r, 0))
-            b = jnp.where(is_l, b_l, jnp.where(used, b_r, 0))
+            used = s < count
+            n = jnp.where(used, jnp.where(is_l, count - 1 - s, s), 0)
+            j = n + jnp.where(is_l, 0, h)
+            start = jnp.where(is_l, ROWS + (n + 1) * na * BLK - ROWS, ROWS + n * nb * BLK)
+            start = jnp.where(used, start, ROWS + SIZE)
+            a, b = jnp.where(used, a_all, 0), jnp.where(used, b_all, 0)
             ok = jnp.logical_or(rows >= ROWS - a, rows < b)
             ok_c = jnp.logical_or(cols_id >= ROWS - a, cols_id < b)
             low = jnp.where(is_l, ROWS - a, 0)
@@ -249,14 +230,10 @@
         return 0
 
     lax.fori_loop(0, (count + BATCH - 1) // BATCH, group, 0)
-    if not second:
-        to_prev[...] = out_pad[left : left + size, :]
-        to_next[...] = out_pad[right : right + size, :]
+    back[...] = out_pad[ROWS : ROWS + SIZE, :]
+    if x == 0:
         gains_ref[...] = sums[...]
         return
-    for out_ref, start, first in ((to_prev, left, first_prev), (to_next, right, first_next)):
-        out_ref[:FIRST, :] = first[...]
-        out_ref[FIRST:, :] = out_pad[start : start + size, :]
     both = jnp.concatenate(
         [
             jnp.sum(sums[0:8, :], axis=0, keepdims=True) / q_gain,
@@ -267,34 +244,36 @@
     gains_ref[...] = jnp.broadcast_to(both[None], gains_ref.shape)
 
 
-def merge_kernel(heads, prm_ref, from_prev, from_next, *refs):
+def merge_kernel(heads, prm_ref, done, done2, *refs):
     local, final, pad = refs[0:4], refs[4:8], refs[8]
     step = pl.program_id(0)
-
-    left, right, _, _ = padded(FIRST + SECOND)
+    bases = (ROWS, 2 * ROWS + SIZE)
 
     @pl.when(step == 0)
     def _():
-        pad[left : left + FIRST + SECOND, :] = from_prev[...]
-        pad[right : right + FIRST + SECOND, :] = from_next[...]
+        for base, ref in zip(bases, (done, done2)):
+            pad[base : base + SIZE, :] = ref[...]
 
     rows = row_ids()
-    _, b, _, nb, h, _, _, one = [prm_ref[i] for i in range(8)]
-    a, _, na, _, h2, _, one2, _ = [prm_ref[8 + i] for i in range(8)]
     each = local[0].shape[1] // HD
     for u in range(each):
         j = step * each + u
-        lead = rows < b * jnp.where(j >= h, 1, 0)
-        tail = rows >= ROWS - a * jnp.where(j < h2, 1, 0)
-        n, n2 = jnp.maximum(j - h, 0), jnp.minimum(j, jnp.maximum(h2 - 1, 0))
-        at = left + jnp.where(n < one, n * nb * BLK, FIRST + (n - one) * nb * BLK)
-        at2 = right + jnp.where(n2 < one2, n2 + 1, n2 + 1 - one2) * na * BLK - ROWS + jnp.where(n2 < one2, 0, FIRST)
-        win_l, win_r = pl.ds(pl.multiple_of(at, BLK), ROWS), pl.ds(pl.multiple_of(at2, BLK), ROWS)
         cols = slice(u * HD, (u + 1) * HD)
+        parts = []
+        for x, base in enumerate(bases):
+            is_left, a, b, na, nb, h, _ = [prm_ref[8 * x + i] for i in range(7)]
+            is_l = is_left == 1
+            sent = jnp.where(is_l, j - h, h - 1 - j) >= 0
+            n = jnp.where(sent, jnp.where(is_l, j - h, j + 1), 0)
+            at = base + jnp.where(is_l, n * nb * BLK, n * na * BLK - ROWS)
+            low = jnp.where(is_l, 0, ROWS - a)
+            high = jnp.where(sent, jnp.where(is_l, b, ROWS), 0)
+            parts.append((pl.ds(pl.multiple_of(at, BLK), ROWS), jnp.logical_and(rows >= low, rows < high)))
         for t in range(4):
-            lanes = slice(t * HD, (t + 1) * HD)
-            value = jnp.where(lead, pad[win_l, lanes], local[t][:, cols])
-            final[t][:, cols] = jnp.where(tail, pad[win_r, lanes], value)
+            value = local[t][:, cols]
+            for window, mask in parts:
+                value = jnp.where(mask, pad[window, t * HD : (t + 1) * HD], value)
+            final[t][:, cols] = value
 
 
 VM = pl.BlockSpec(memory_space=pltpu.VMEM)
@@ -334,61 +313,51 @@
     seg = segments[0].reshape(ring, rows)
     gains = (q_gain.reshape(1, HD), k_gain.reshape(1, HD))
     full = jax.ShapeDtypeStruct((rows, width), BF16)
-    sent, sent2, back = [jax.ShapeDtypeStruct((n, 4 * HD), BF16) for n in (FIRST, SECOND, FIRST + SECOND)]
+    sent = jax.ShapeDtypeStruct((SIZE, 4 * HD), BF16)
     part = jax.ShapeDtypeStruct((16, HD), F32)
-    up = [(i, i + 1) for i in range(ring - 1)]
-    down = [(i + 1, i) for i in range(ring - 1)]
-
-    def pad(size):
-        return pltpu.VMEM((padded(size)[3], 4 * HD), BF16)
-
-    to_prev, to_next, to_prev2, to_next2, prm, *args, seg = call(
+    pad = pltpu.VMEM((SIZE + 2 * ROWS, 4 * HD), BF16)
+    even, odd = [[(i, i + 1) for i in range(x, ring - 1, 2)] + [(i + 1, i) for i in range(x, ring - 1, 2)] for x in range(2)]
+
+    out, out2, prm, *args, seg = call(
         functools.partial(pack_kernel, heads),
         [HB] * 5,
-        [VM] * 4 + [SM] + [VM] * 5,
-        [sent, sent, sent2, sent2, jax.ShapeDtypeStruct((16,), jnp.int32)]
-        + [full] * 4
-        + [jax.ShapeDtypeStruct(seg.shape, seg.dtype)],
+        [VM, VM, SM] + [VM] * 5,
+        [sent, sent, jax.ShapeDtypeStruct((16,), jnp.int32)] + [full] * 4 + [jax.ShapeDtypeStruct(seg.shape, seg.dtype)],
         1 << 20,
         [pltpu.SemaphoreType.DMA((17,))],
         vmem=12,
     )(*[pltpu.with_memory_space_constraint(x, pltpu.HBM) for x in (*args, seg)])
-    from_prev = lax.ppermute(to_next, "tp", up)
-    from_next = lax.ppermute(to_prev, "tp", down)
-    from_prev2 = lax.ppermute(to_next2, "tp", up)
-    from_next2 = lax.ppermute(to_prev2, "tp", down)
+    received = lax.ppermute(out, "tp", even)
+    received2 = lax.ppermute(out2, "tp", odd)
     *local, sums = local_call(heads, (prm, *args, seg, *gains))
-    *merged, first_prev, first_next, sums = call(
-        functools.partial(cross_kernel, heads, False),
-        [SM] + [VM] * 13,
-        [VM] * 7,
-        [full] * 4 + [sent, sent, part],
-        1 << 30,
-        [pad(FIRST), pad(FIRST), pltpu.VMEM((16, HD), F32)],
-    )(prm, *args, from_prev, from_next, *gains, sums, *local)
-    *merged, back_prev, back_next, sums = call(
-        functools.partial(cross_kernel, heads, True),
-        [SM] + [VM] * 15,
-        [VM] * 7,
-        [full] * 4 + [back, back, jax.ShapeDtypeStruct((groups, 2, HD), F32)],
-        1 << 30,
-        [pad(SECOND), pad(SECOND), pltpu.VMEM((16, HD), F32)],
-    )(prm, *args, from_prev2, from_next2, *gains, sums, *merged, first_prev, first_next)
-    done_next = lax.ppermute(back_prev, "tp", down)
-    done_prev = lax.ppermute(back_next, "tp", up)
+
+    def cross(x, received, sums, local):
+        return call(
+            functools.partial(cross_kernel, heads, x),
+            [SM] + [VM] * 12,
+            [VM] * 6,
+            [full] * 4 + [sent, jax.ShapeDtypeStruct((groups, 2, HD), F32) if x else part],
+            1 << 30,
+            [pad, pad, pltpu.VMEM((16, HD), F32)],
+        )(prm, *args, received, *gains, sums, *local)
+
+    *merged, back, sums = cross(0, received, sums, local)
+    done = lax.ppermute(back, "tp", even)
+    *merged, back2, sums = cross(1, received2, sums, merged)
+    done2 = lax.ppermute(back2, "tp", odd)
     sums = jnp.sum(lax.all_to_all(sums, "grp", 0, 0), axis=0)
     block = pl.BlockSpec((rows, width // 4), lambda i: (0, i))
-    whole = pl.BlockSpec((FIRST + SECOND, 4 * HD), lambda i: (0, 0))
+    whole = pl.BlockSpec((SIZE, 4 * HD), lambda i: (0, 0))
     outs = call(
         functools.partial(merge_kernel, heads),
         [SM, whole, whole] + [block] * 4,
         [block] * 4,
         [full] * 4,
         1 << 20,
-        [pad(FIRST + SECOND)],
+        [pltpu.VMEM((2 * SIZE + 3 * ROWS, 4 * HD), BF16)],
         (4,),
         16,
-    )(prm, done_prev, done_next, *merged)
+    )(prm, done, done2, *merged)
     sums = jnp.sum(lax.all_to_all(jnp.broadcast_to(sums, (ring, 2, HD)), "tp", 0, 0), axis=0)
     gain_grads = sums * (1.0 / math.sqrt(groups * ring * rows * heads))
     return tuple(x[None] for x in outs) + (gain_grads,)

time: 84.1 us -> 81.6 us (0.970)
  blocking collectives: 48.5 us -> 43.8 us
  Pallas kernels: 16.1 us -> 12.3 us
  starting transfers between devices: 16 us -> 19.8 us
  waiting for transfers between devices: 1.13 us -> 3.35 us
    all_to_all x1, blocking collectives: 30.5 us -> 23.4 us  [per_device(): lax.all_to_all(jnp.broadcast_to(sums, (ring, 2, HD)), 'tp', 0, 0)]
    pallas_call x3, Pallas kernels: 9.57 us -> 5.52 us  [the longest x2 3.16 us: cross(): call(functools.partial(cross_kernel, heads, x), [SM] + [VM] * 12, [VM] *...]
    ppermute x6 -> x4, starting transfers between devices: 16 us -> 19.8 us  [the longest x1 14.1 us: per_device(): done = lax.ppermute(back, 'tp', even)]
    all_to_all x1, blocking collectives: 18 us -> 20.4 us  [per_device(): sums = jnp.sum(lax.all_to_all(sums, 'grp', 0, 0), axis=0)]
    ppermute x6 -> x4, waiting for transfers between devices: 1.13 us -> 3.35 us  [the longest x1 3.35 us: per_device(): received = lax.ppermute(out, 'tp', even)]
  transfers between devices with their start and end apart: 6 -> 4, of which waited for: 1 -> 1; matrix products, arithmetic and copies ran while one was open for 1% -> 1% of each run, Pallas kernels for 8% -> 6%
where the time goes in v3:
time: 81.6 us; the launch traced here: 81.3 us
  blocking collectives  43.8 us (54%)
  starting transfers between devices  19.8 us (24%)
  Pallas kernels  12.3 us (15%)
  waiting for transfers between devices  3.35 us (4%)
    all_to_all x1, blocking collectives, per_device(): lax.all_to_all(jnp.broadcast_to(sums, (ring, 2, HD)), 'tp', 0, 0)  23.4 us
    all_to_all x1, blocking collectives, per_device(): sums = jnp.sum(lax.all_to_all(sums, 'grp', 0, 0), axis=0)  20.4 us
    ppermute x1, starting transfers between devices, per_device(): done = lax.ppermute(back, 'tp', even)  14.1 us
    ppermute x1, starting transfers between devices, per_device(): received = lax.ppermute(out, 'tp', even)  4.38 us
    pallas_call x1, Pallas kernels, local_call(): call(functools.partial(local_kernel, heads, 1.0 / math.sqrt(HD)), [SM] +...  3.39 us
    pallas_call x1, Pallas kernels, per_device(): call(functools.partial(merge_kernel, heads), [SM, whole, whole] + [block]...  3.35 us
    ppermute x1, waiting for transfers between devices, per_device(): received = lax.ppermute(out, 'tp', even)  3.35 us
    pallas_call x2, Pallas kernels, cross(): call(functools.partial(cross_kernel, heads, x), [SM] + [VM] * 12, [VM] *...  3.16 us
  transfers between devices with their start and end apart: 4, of which 1 were waited for; matrix products, arithmetic and copies ran while one was open for 1% of the time, Pallas kernels for 6%

profile of v3, /device:TPU:1, one launch (start us, length us, event | category | flops | bytes accessed | tf_op | source)
XLA Modules:
  0.0 81.3 jit_solution(385203527903501321)
XLA Ops:
  0.6 2.4 %shard_map.110 = (bf16[576,512]{1,0:T(8,128)(2,1)S(1)}, bf16[576,512]{1,0:T(8,128)(2,1)S(1)}, s32[16]{0:T(128)S(1)}, bf16[128,2048]{1,0:T(8,128)(2,1)S(1)}, bf16...) custom-call(bf16[128,2048]{1,0:T(8,128)(2,1)} %bitcast.17, ...), custom_call_target="tpu_custom_call" | custom-call | flops 1048576 | bytes 4194304 | tf_op jit(solution)/shard_map/pallas_call | solution.py:321
  3.0 4.4 %collective-permute-start = (bf16[576,512]{1,0:T(8,128)(2,1)S(1)}, bf16[576,512]{1,0:T(8,128)(2,1)S(1)}, u32[]{:S(2)}, u32[]{:S(2)}) collective-permute-start(bf16[576,512]{1,0:T(8,128)(2,1)S(1)} %get-tuple-element.39), channel_id=1, source_target_pairs={{0,1},{2,3},{4,5},{6,7},{8,9},{10,11},{12,13},{14,15},{1,0},{3,2},... | collective-permute-start | bytes 1769480 | tf_op jit(solution)/shard_map/ppermute | solution.py:330
  7.4 0.7 collective-permute-start.2
  8.1 0.0 copy-start
  8.1 0.0 copy-start.1
  8.1 0.6 copy-done
  8.7 0.0 copy-done.1
  8.8 3.4 %shard_map.111 = (bf16[128,2048]{1,0:T(8,128)(2,1)S(1)}, bf16[128,2048]{1,0:T(8,128)(2,1)S(1)}, bf16[128,2048]{1,0:T(8,128)(2,1)S(1)}, bf16[128,2048]{1,0:T(8,128)(2,1)S(1)}, f32[16,128]{1,0:T(8,128)S(1)}) custom-call(s32[16]{0:T(128)S(1)} %get-tuple-element.34.prm_ref, bf16[128,2048]{1,0:T(8,128)(2,1)S(1)} %get-tuple-element.35.q_ref.refs_0_, ...), custom_call_target="tpu_custom_call" | custom-call | flops 1073741824 | bytes 4194304 | tf_op jit(solution)/shard_map/pallas_call | solution.py:299
  12.2 3.3 %collective-permute-done.refs_4_ = bf16[576,512]{1,0:T(8,128)(2,1)S(1)} collective-permute-done((bf16[576,512]{1,0:T(8,128)(2,1)S(1)}, bf16[576,512]{1,0:T(8,128)(2,1)S(1)}, u32[]{:S(2)}, u32[]{:S(2)}) %collective-permute-start) | collective-permute-done | bytes 589856 | tf_op jit(solution)/shard_map/ppermute | solution.py:330
  15.5 1.6 %shard_map.112 = (bf16[128,2048]{1,0:T(8,128)(2,1)S(1)}, bf16[128,2048]{1,0:T(8,128)(2,1)S(1)}, bf16[128,2048]{1,0:T(8,128)(2,1)S(1)}, bf16[128,2048]{1,0:T(8,12...) custom-call(s32[16]{0:T(128)S(1)} %get-tuple-element.34.prm_ref, ...), custom_call_target="tpu_custom_call" | custom-call | flops 1073741824 | bytes 4194304 | tf_op jit(solution)/shard_map/pallas_call | solution.py:335
  17.1 0.0 collective-permute-done.2.refs_4_
  17.1 1.6 %shard_map.113 = (bf16[128,2048]{1,0:T(8,128)(2,1)S(1)}, bf16[128,2048]{1,0:T(8,128)(2,1)S(1)}, bf16[128,2048]{1,0:T(8,128)(2,1)S(1)}, bf16[128,2048]{1,0:T(8,12...) custom-call(s32[16]{0:T(128)S(1)} %get-tuple-element.34.prm_ref, ...), custom_call_target="tpu_custom_call" | custom-call | flops 1073741824 | bytes 4194304 | tf_op jit(solution)/shard_map/pallas_call | solution.py:335
  18.7 0.7 collective-permute-start.3
  19.4 14.1 %collective-permute-start.1 = (bf16[576,512]{1,0:T(8,128)(2,1)}, bf16[576,512]{1,0:T(8,128)(2,1)S(1)}, u32[]{:S(2)}, u32[]{:S(2)}) collective-permute-start(bf16[576,512]{1,0:T(8,128)(2,1)} %get-tuple-element.46), channel_id=1, source_target_pairs={{0,1},{2,3},{4,5},{6,7},{8,9},{10,11},{12,13},{14,15},{1,0},{3,2},... | collective-permute-start | bytes 1769480 | tf_op jit(solution)/shard_map/ppermute | solution.py:345
  33.4 20.4 %all_to_all.10 = f32[32,2,128]{2,1,0:T(2,128)S(1)} all-to-all(f32[32,2,128]{2,1,0:T(2,128)S(1)} %get-tuple-element.62), channel_id=1, replica_groups=mesh['grp'=32,'tp'=16] {'grp'}, dimensions={0} | all-to-all | bytes 65536 | tf_op jit(solution)/shard_map/all_to_all | solution.py:348
  53.9 23.4 %all_to_all.11 = f32[16,2,128]{2,1,0:T(2,128)S(1)} all-to-all(f32[16,2,128]{2,1,0:T(2,128)S(1)} %broadcast_in_dim.19), channel_id=1, replica_groups=mesh['grp'=32,'tp'=16] {'tp'}, dimensions={0} | all-to-all | bytes 32768 | tf_op jit(solution)/shard_map/all_to_all | solution.py:361
  77.3 0.6 broadcast_multiply_fusion
  77.9 0.0 collective-permute-done.3.done2
  77.9 0.0 collective-permute-done.1.done
  77.9 3.4 %shard_map.114 = (bf16[128,2048]{1,0:T(8,128)(2,1)}, bf16[128,2048]{1,0:T(8,128)(2,1)}, bf16[128,2048]{1,0:T(8,128)(2,1)}, bf16[128,2048]{1,0:T(8,128)(2,1)}) custom-call(s32[16]{0:T(128)S(1)} %get-tuple-element.34.prm_ref, bf16[576,512]{1,0:T(8,128)(2,1)S(1)} %collective-permute-done.1.done, bf16[576,512]{1,0:T(8,128)(2,1)S(1)} %collective-permute-done.3.done2, ...), custom_call_target="tpu_custom_call" | custom-call | flops 1048576 | bytes 4194304 | tf_op jit(solution)/shard_map/pallas_call | solution.py:351
  (3 shorter events, 0.1 us)
Async XLA Ops:
  3.0 12.5 %collective-permute-start = (bf16[576,512]{1,0:T(8,128)(2,1)S(1)}, bf16[576,512]{1,0:T(8,128)(2,1)S(1)}, u32[]{:S(2)}, u32[]{:S(2)}) collective-permute-start(bf16[576,512]{1,0:T(8,128)(2,1)S(1)} %get-tuple-element.39), channel_id=1, source_target_pairs={{0,1},{2,3},{4,5},{6,7},{8,9},{10,11},{12,13},{14,15},{1,0},{3,2},... | collective-permute-start | bytes 1769480 | tf_op jit(solution)/shard_map/ppermute | solution.py:330
  7.4 9.7 %collective-permute-start.2 = (bf16[576,512]{1,0:T(8,128)(2,1)S(1)}, bf16[576,512]{1,0:T(8,128)(2,1)S(1)}, u32[]{:S(2)}, u32[]{:S(2)}) collective-permute-start(bf16[576,512]{1,0:T(8,128)(2,1)S(1)} %get-tuple-element.47), channel_id=1, source_target_pairs={{1,2},{3,4},{5,6},{7,8},{9,10},{11,12},{13,14},{2,1},{4,3},{6,5},{... | collective-permute-start | bytes 1769480 | tf_op jit(solution)/shard_map/ppermute | solution.py:331
  8.1 0.7 copy-start
  8.1 0.7 copy-start.1
  18.7 59.2 %collective-permute-start.3 = (bf16[576,512]{1,0:T(8,128)(2,1)}, bf16[576,512]{1,0:T(8,128)(2,1)S(1)}, u32[]{:S(2)}, u32[]{:S(2)}) collective-permute-start(bf16[576,512]{1,0:T(8,128)(2,1)} %get-tuple-element.53), channel_id=1, source_target_pairs={{1,2},{3,4},{5,6},{7,8},{9,10},{11,12},{13,14},{2,1},{4,3},{6,5},{... | collective-permute-start | bytes 1769480 | tf_op jit(solution)/shard_map/ppermute | solution.py:347
  19.4 58.6 %collective-permute-start.1 = (bf16[576,512]{1,0:T(8,128)(2,1)}, bf16[576,512]{1,0:T(8,128)(2,1)S(1)}, u32[]{:S(2)}, u32[]{:S(2)}) collective-permute-start(bf16[576,512]{1,0:T(8,128)(2,1)} %get-tuple-element.46), channel_id=1, source_target_pairs={{0,1},{2,3},{4,5},{6,7},{8,9},{10,11},{12,13},{14,15},{1,0},{3,2},... | collective-permute-start | bytes 1769480 | tf_op jit(solution)/shard_map/ppermute | solution.py:345

commit v4 on v3

--- a/solution.py
+++ b/solution.py
@@ -12,6 +12,7 @@
 ROWS = 128
 BLK = 16
 BATCH = 8
+MOST = 12
 CAP = 36
 SIZE = CAP * BLK
 MIB = 1024 * 1024
@@ -197,10 +198,9 @@
     is_l = is_left == 1
     count = jnp.where(is_l, h, rest)
 
-    def group(i, _):
+    def work(windows):
         items, places = [], []
-        for u in range(BATCH):
-            s = i * BATCH + u
+        for s in range(windows):
             used = s < count
             n = jnp.where(used, jnp.where(is_l, count - 1 - s, s), 0)
             j = n + jnp.where(is_l, 0, h)
@@ -227,9 +227,15 @@
                 out_pad[window, t * HD : (t + 1) * HD] = value
         sums[0:8, :] += fold(sum(gq))
         sums[8:16, :] += fold(sum(gk))
-        return 0
-
-    lax.fori_loop(0, (count + BATCH - 1) // BATCH, group, 0)
+
+    @pl.when(jnp.logical_and(count > 0, count <= BATCH))
+    def _():
+        work(BATCH)
+
+    @pl.when(count > BATCH)
+    def _():
+        work(MOST)
+
     back[...] = out_pad[ROWS : ROWS + SIZE, :]
     if x == 0:
         gains_ref[...] = sums[...]
@@ -276,6 +282,10 @@
             final[t][:, cols] = value
 
 
+def total_kernel(scale, parts_ref, after_ref, out_ref):
+    out_ref[...] = jnp.sum(parts_ref[...], axis=0) * scale
+
+
 VM = pl.BlockSpec(memory_space=pltpu.VMEM)
 SM = pl.BlockSpec(memory_space=pltpu.SMEM)
 HB = pl.BlockSpec(memory_space=pltpu.HBM)
@@ -358,8 +368,15 @@
         (4,),
         16,
     )(prm, done, done2, *merged)
-    sums = jnp.sum(lax.all_to_all(jnp.broadcast_to(sums, (ring, 2, HD)), "tp", 0, 0), axis=0)
-    gain_grads = sums * (1.0 / math.sqrt(groups * ring * rows * heads))
+    sums = lax.all_to_all(jnp.broadcast_to(sums, (ring, 2, HD)), "tp", 0, 0)
+    gain_grads = call(
+        functools.partial(total_kernel, 1.0 / math.sqrt(groups * ring * rows * heads)),
+        [VM, HB],
+        VM,
+        jax.ShapeDtypeStruct((2, HD), F32),
+        1 << 10,
+        vmem=4,
+    )(sums, pltpu.with_memory_space_constraint(outs[0], pltpu.HBM))
     return tuple(x[None] for x in outs) + (gain_grads,)
 
 

time: 81.6 us -> 78.7 us (0.964)
  blocking collectives: 43.8 us -> 16.9 us
  starting transfers between devices: 19.8 us -> 30.6 us
  waiting for transfers between devices: 3.35 us -> 12.1 us
  Pallas kernels: 12.3 us -> 16.8 us
    all_to_all x1 -> x0, blocking collectives: 23.4 us -> none  [per_device(): lax.all_to_all(jnp.broadcast_to(sums, (ring, 2, HD)), 'tp', 0, 0)]
    all_to_all x0 -> x1, starting transfers between devices: none -> 12.9 us  [per_device(): sums = lax.all_to_all(jnp.broadcast_to(sums, (ring, 2, HD)), 'tp', 0, 0)]
    all_to_all x0 -> x1, waiting for transfers between devices: none -> 8 us  [per_device(): sums = lax.all_to_all(jnp.broadcast_to(sums, (ring, 2, HD)), 'tp', 0, 0)]
    all_to_all x1, blocking collectives: 20.4 us -> 16.9 us  [per_device(): sums = jnp.sum(lax.all_to_all(sums, 'grp', 0, 0), axis=0)]
    pallas_call x2, Pallas kernels: 3.16 us -> 6.65 us  [cross(): call(functools.partial(cross_kernel, heads, x), [SM] + [VM] * 12, [VM] *...]
    ppermute x1, starting transfers between devices: 14.1 us -> 11.5 us  [per_device(): done = lax.ppermute(back, 'tp', even)]
  transfers between devices with their start and end apart: 4 -> 5, of which waited for: 1 -> 2; matrix products, arithmetic and copies ran while one was open for 1% -> 1% of each run, Pallas kernels for 6% -> 15%
where the time goes in v4:
time: 78.7 us; the launch traced here: 78.4 us
  starting transfers between devices  30.6 us (39%)
  blocking collectives  16.9 us (21%)
  Pallas kernels  16.8 us (21%)
  waiting for transfers between devices  12.1 us (15%)
  local copies, waits for them, and re-layouts  1.27 us (2%)
    all_to_all x1, blocking collectives, per_device(): sums = jnp.sum(lax.all_to_all(sums, 'grp', 0, 0), axis=0)  16.9 us
    all_to_all x1, starting transfers between devices, per_device(): sums = lax.all_to_all(jnp.broadcast_to(sums, (ring, 2, HD)), 'tp', 0, 0)  12.9 us
    ppermute x1, starting transfers between devices, per_device(): done = lax.ppermute(back, 'tp', even)  11.5 us
    all_to_all x1, waiting for transfers between devices, per_device(): sums = lax.all_to_all(jnp.broadcast_to(sums, (ring, 2, HD)), 'tp', 0, 0)  8 us
    pallas_call x2, Pallas kernels, cross(): call(functools.partial(cross_kernel, heads, x), [SM] + [VM] * 12, [VM] *...  6.65 us
    ppermute x1, starting transfers between devices, per_device(): received = lax.ppermute(out, 'tp', even)  4.81 us
    ppermute x1, waiting for transfers between devices, per_device(): received = lax.ppermute(out, 'tp', even)  4.13 us
    pallas_call x1, Pallas kernels, local_call(): call(functools.partial(local_kernel, heads, 1.0 / math.sqrt(HD)), [SM] +...  3.38 us
  transfers between devices with their start and end apart: 5, of which 2 were waited for; matrix products, arithmetic and copies ran while one was open for 1% of the time, Pallas kernels for 15%

profile of v4, /device:TPU:1, one launch (start us, length us, event | category | flops | bytes accessed | tf_op | source)
XLA Modules:
  0.0 78.4 jit_solution(16336873041662811870)
XLA Ops:
  0.6 2.8 %shard_map.110 = (bf16[576,512]{1,0:T(8,128)(2,1)S(1)}, bf16[576,512]{1,0:T(8,128)(2,1)S(1)}, s32[16]{0:T(128)S(1)}, bf16[128,2048]{1,0:T(8,128)(2,1)S(1)}, bf16...) custom-call(bf16[128,2048]{1,0:T(8,128)(2,1)} %bitcast.18, ...), custom_call_target="tpu_custom_call" | custom-call | flops 1048576 | bytes 4194304 | tf_op jit(solution)/shard_map/pallas_call | solution.py:331
  3.4 4.8 %collective-permute-start = (bf16[576,512]{1,0:T(8,128)(2,1)S(1)}, bf16[576,512]{1,0:T(8,128)(2,1)S(1)}, u32[]{:S(2)}, u32[]{:S(2)}) collective-permute-start(bf16[576,512]{1,0:T(8,128)(2,1)S(1)} %get-tuple-element.39), channel_id=1, source_target_pairs={{0,1},{2,3},{4,5},{6,7},{8,9},{10,11},{12,13},{14,15},{1,0},{3,2},... | collective-permute-start | bytes 1769480 | tf_op jit(solution)/shard_map/ppermute | solution.py:340
  8.2 0.7 collective-permute-start.2
  8.9 0.0 copy-start
  8.9 0.0 copy-start.1
  9.0 0.6 copy-done
  9.6 0.0 copy-done.1
  9.6 3.4 %shard_map.111 = (bf16[128,2048]{1,0:T(8,128)(2,1)S(1)}, bf16[128,2048]{1,0:T(8,128)(2,1)S(1)}, bf16[128,2048]{1,0:T(8,128)(2,1)S(1)}, bf16[128,2048]{1,0:T(8,128)(2,1)S(1)}, f32[16,128]{1,0:T(8,128)S(1)}) custom-call(s32[16]{0:T(128)S(1)} %get-tuple-element.34.prm_ref, bf16[128,2048]{1,0:T(8,128)(2,1)S(1)} %get-tuple-element.35.q_ref.refs_0_, ...), custom_call_target="tpu_custom_call" | custom-call | flops 1073741824 | bytes 4194304 | tf_op jit(solution)/shard_map/pallas_call | solution.py:309
  13.0 4.1 %collective-permute-done.refs_4_ = bf16[576,512]{1,0:T(8,128)(2,1)S(1)} collective-permute-done((bf16[576,512]{1,0:T(8,128)(2,1)S(1)}, bf16[576,512]{1,0:T(8,128)(2,1)S(1)}, u32[]{:S(2)}, u32[]{:S(2)}) %collective-permute-start) | collective-permute-done | bytes 589856 | tf_op jit(solution)/shard_map/ppermute | solution.py:340
  17.1 4.9 %shard_map.112 = (bf16[128,2048]{1,0:T(8,128)(2,1)S(1)}, bf16[128,2048]{1,0:T(8,128)(2,1)S(1)}, bf16[128,2048]{1,0:T(8,128)(2,1)S(1)}, bf16[128,2048]{1,0:T(8,12...) custom-call(s32[16]{0:T(128)S(1)} %get-tuple-element.34.prm_ref, ...), custom_call_target="tpu_custom_call" | custom-call | flops 1073741824 | bytes 4194304 | tf_op jit(solution)/shard_map/pallas_call | solution.py:345
  22.0 0.0 collective-permute-done.2.refs_4_
  22.0 1.8 %shard_map.113 = (bf16[128,2048]{1,0:T(8,128)(2,1)S(1)}, bf16[128,2048]{1,0:T(8,128)(2,1)S(1)}, bf16[128,2048]{1,0:T(8,128)(2,1)S(1)}, bf16[128,2048]{1,0:T(8,12...) custom-call(s32[16]{0:T(128)S(1)} %get-tuple-element.34.prm_ref, ...), custom_call_target="tpu_custom_call" | custom-call | flops 1073741824 | bytes 4194304 | tf_op jit(solution)/shard_map/pallas_call | solution.py:345
  23.8 0.7 collective-permute-start.3
  24.5 11.5 %collective-permute-start.1 = (bf16[576,512]{1,0:T(8,128)(2,1)}, bf16[576,512]{1,0:T(8,128)(2,1)S(1)}, u32[]{:S(2)}, u32[]{:S(2)}) collective-permute-start(bf16[576,512]{1,0:T(8,128)(2,1)} %get-tuple-element.46), channel_id=1, source_target_pairs={{0,1},{2,3},{4,5},{6,7},{8,9},{10,11},{12,13},{14,15},{1,0},{3,2},... | collective-permute-start | bytes 1769480 | tf_op jit(solution)/shard_map/ppermute | solution.py:355
  35.9 16.9 %all_to_all.10 = f32[32,2,128]{2,1,0:T(2,128)S(1)} all-to-all(f32[32,2,128]{2,1,0:T(2,128)S(1)} %get-tuple-element.62), channel_id=1, replica_groups=mesh['grp'=32,'tp'=16] {'grp'}, dimensions={0} | all-to-all | bytes 65536 | tf_op jit(solution)/shard_map/all_to_all | solution.py:358
  52.9 0.6 broadcast_in_dim.19
  53.5 12.9 %all-to-all-start.1 = ((f32[16,2,128]{2,1,0:T(2,128)}), f32[16,2,128]{2,1,0:T(2,128)S(1)}, u32[]{:S(2)}, u32[]{:S(2)}) async-start(f32[16,2,128]{2,1,0:T(2,128)} %broadcast_in_dim.19), calls=%async_computation.1 | async-start | bytes 32768 | tf_op jit(solution)/shard_map/all_to_all | solution.py:371
  66.4 0.0 collective-permute-done.3.done2
  66.4 0.0 collective-permute-done.1.done
  66.4 3.4 %shard_map.114 = (bf16[128,2048]{1,0:T(8,128)(2,1)}, bf16[128,2048]{1,0:T(8,128)(2,1)}, bf16[128,2048]{1,0:T(8,128)(2,1)}, bf16[128,2048]{1,0:T(8,128)(2,1)}) custom-call(s32[16]{0:T(128)S(1)} %get-tuple-element.34.prm_ref, bf16[576,512]{1,0:T(8,128)(2,1)S(1)} %collective-permute-done.1.done, bf16[576,512]{1,0:T(8,128)(2,1)S(1)} %collective-permute-done.3.done2, ...), custom_call_target="tpu_custom_call" | custom-call | flops 1048576 | bytes 4194304 | tf_op jit(solution)/shard_map/pallas_call | solution.py:361
  69.8 8.0 %all-to-all-done.1.parts_ref = f32[16,2,128]{2,1,0:T(2,128)S(1)} async-done(((f32[16,2,128]{2,1,0:T(2,128)}), f32[16,2,128]{2,1,0:T(2,128)S(1)}, u32[]{:S(2)}, u32[]{:S(2)}) %all-to-all-start.1) | async-done | bytes 16416 | tf_op jit(solution)/shard_map/all_to_all | solution.py:371
  77.8 0.6 shard_map.115
  (1 shorter events, 0.0 us)
Async XLA Ops:
  3.4 13.7 %collective-permute-start = (bf16[576,512]{1,0:T(8,128)(2,1)S(1)}, bf16[576,512]{1,0:T(8,128)(2,1)S(1)}, u32[]{:S(2)}, u32[]{:S(2)}) collective-permute-start(bf16[576,512]{1,0:T(8,128)(2,1)S(1)} %get-tuple-element.39), channel_id=1, source_target_pairs={{0,1},{2,3},{4,5},{6,7},{8,9},{10,11},{12,13},{14,15},{1,0},{3,2},... | collective-permute-start | bytes 1769480 | tf_op jit(solution)/shard_map/ppermute | solution.py:340
  8.2 13.8 %collective-permute-start.2 = (bf16[576,512]{1,0:T(8,128)(2,1)S(1)}, bf16[576,512]{1,0:T(8,128)(2,1)S(1)}, u32[]{:S(2)}, u32[]{:S(2)}) collective-permute-start(bf16[576,512]{1,0:T(8,128)(2,1)S(1)} %get-tuple-element.47), channel_id=1, source_target_pairs={{1,2},{3,4},{5,6},{7,8},{9,10},{11,12},{13,14},{2,1},{4,3},{6,5},{... | collective-permute-start | bytes 1769480 | tf_op jit(solution)/shard_map/ppermute | solution.py:341
  8.9 0.7 copy-start
  8.9 0.7 copy-start.1
  23.8 42.6 %collective-permute-start.3 = (bf16[576,512]{1,0:T(8,128)(2,1)}, bf16[576,512]{1,0:T(8,128)(2,1)S(1)}, u32[]{:S(2)}, u32[]{:S(2)}) collective-permute-start(bf16[576,512]{1,0:T(8,128)(2,1)} %get-tuple-element.53), channel_id=1, source_target_pairs={{1,2},{3,4},{5,6},{7,8},{9,10},{11,12},{13,14},{2,1},{4,3},{6,5},{... | collective-permute-start | bytes 1769480 | tf_op jit(solution)/shard_map/ppermute | solution.py:357
  24.5 41.9 %collective-permute-start.1 = (bf16[576,512]{1,0:T(8,128)(2,1)}, bf16[576,512]{1,0:T(8,128)(2,1)S(1)}, u32[]{:S(2)}, u32[]{:S(2)}) collective-permute-start(bf16[576,512]{1,0:T(8,128)(2,1)} %get-tuple-element.46), channel_id=1, source_target_pairs={{0,1},{2,3},{4,5},{6,7},{8,9},{10,11},{12,13},{14,15},{1,0},{3,2},... | collective-permute-start | bytes 1769480 | tf_op jit(solution)/shard_map/ppermute | solution.py:355
  53.5 24.3 %all-to-all-start.1 = ((f32[16,2,128]{2,1,0:T(2,128)}), f32[16,2,128]{2,1,0:T(2,128)S(1)}, u32[]{:S(2)}, u32[]{:S(2)}) async-start(f32[16,2,128]{2,1,0:T(2,128)} %broadcast_in_dim.19), calls=%async_computation.1 | async-start | bytes 32768 | tf_op jit(solution)/shard_map/all_to_all | solution.py:371

commit v5 on v4

--- a/solution.py
+++ b/solution.py
@@ -367,7 +367,7 @@
         [pltpu.VMEM((2 * SIZE + 3 * ROWS, 4 * HD), BF16)],
         (4,),
         16,
-    )(prm, done, done2, *merged)
+    )(prm, *[pltpu.with_memory_space_constraint(x, pltpu.HBM) for x in (done, done2)], *merged)
     sums = lax.all_to_all(jnp.broadcast_to(sums, (ring, 2, HD)), "tp", 0, 0)
     gain_grads = call(
         functools.partial(total_kernel, 1.0 / math.sqrt(groups * ring * rows * heads)),

time: 78.7 us -> 77.3 us (0.982)
  starting transfers between devices: 30.6 us -> 32.8 us
  Pallas kernels: 16.8 us -> 14.7 us
  blocking collectives: 16.9 us -> 15.9 us
    pallas_call x2, Pallas kernels: 6.65 us -> 3.94 us  [cross(): call(functools.partial(cross_kernel, heads, x), [SM] + [VM] * 12, [VM] *...]
    ppermute x1, starting transfers between devices: 11.5 us -> 12.8 us  [per_device(): done = lax.ppermute(back, 'tp', even)]
    all_to_all x1, blocking collectives: 16.9 us -> 15.9 us  [per_device(): sums = jnp.sum(lax.all_to_all(sums, 'grp', 0, 0), axis=0)]
    ppermute x1, starting transfers between devices: 0.69 us -> 1.49 us  [per_device(): done2 = lax.ppermute(back2, 'tp', odd)]
  transfers between devices with their start and end apart: 5 -> 5, of which waited for: 2 -> 2; matrix products, arithmetic and copies ran while one was open for 1% -> 1% of each run, Pallas kernels for 15% -> 14%
where the time goes in v5:
time: 77.3 us; the launch traced here: 77 us
  starting transfers between devices  32.8 us (42%)
  blocking collectives  15.9 us (21%)
  Pallas kernels  14.7 us (19%)
  waiting for transfers between devices  11.6 us (15%)
  local copies, waits for them, and re-layouts  1.27 us (2%)
    all_to_all x1, blocking collectives, per_device(): sums = jnp.sum(lax.all_to_all(sums, 'grp', 0, 0), axis=0)  15.9 us
    all_to_all x1, starting transfers between devices, per_device(): sums = lax.all_to_all(jnp.broadcast_to(sums, (ring, 2, HD)), 'tp', 0, 0)  13.1 us
    ppermute x1, starting transfers between devices, per_device(): done = lax.ppermute(back, 'tp', even)  12.8 us
    all_to_all x1, waiting for transfers between devices, per_device(): sums = lax.all_to_all(jnp.broadcast_to(sums, (ring, 2, HD)), 'tp', 0, 0)  7.29 us
    ppermute x1, starting transfers between devices, per_device(): received = lax.ppermute(out, 'tp', even)  4.67 us
    ppermute x1, waiting for transfers between devices, per_device(): received = lax.ppermute(out, 'tp', even)  4.3 us
    pallas_call x1, Pallas kernels, per_device(): call(functools.partial(merge_kernel, heads), [SM, whole, whole] + [block]...  4.08 us
    pallas_call x2, Pallas kernels, cross(): call(functools.partial(cross_kernel, heads, x), [SM] + [VM] * 12, [VM] *...  3.94 us
  transfers between devices with their start and end apart: 5, of which 2 were waited for; matrix products, arithmetic and copies ran while one was open for 1% of the time, Pallas kernels for 14%

profile of v5, /device:TPU:1, one launch (start us, length us, event | category | flops | bytes accessed | tf_op | source)
XLA Modules:
  0.0 77.0 jit_solution(12472992630504435174)
XLA Ops:
  0.6 2.7 %shard_map.110 = (bf16[576,512]{1,0:T(8,128)(2,1)S(1)}, bf16[576,512]{1,0:T(8,128)(2,1)S(1)}, s32[16]{0:T(128)S(1)}, bf16[128,2048]{1,0:T(8,128)(2,1)S(1)}, bf16...) custom-call(bf16[128,2048]{1,0:T(8,128)(2,1)} %bitcast.18, ...), custom_call_target="tpu_custom_call" | custom-call | flops 1048576 | bytes 4194304 | tf_op jit(solution)/shard_map/pallas_call | solution.py:331
  3.3 4.7 %collective-permute-start = (bf16[576,512]{1,0:T(8,128)(2,1)S(1)}, bf16[576,512]{1,0:T(8,128)(2,1)S(1)}, u32[]{:S(2)}, u32[]{:S(2)}) collective-permute-start(bf16[576,512]{1,0:T(8,128)(2,1)S(1)} %get-tuple-element.39), channel_id=1, source_target_pairs={{0,1},{2,3},{4,5},{6,7},{8,9},{10,11},{12,13},{14,15},{1,0},{3,2},... | collective-permute-start | bytes 1769480 | tf_op jit(solution)/shard_map/ppermute | solution.py:340
  8.0 0.7 collective-permute-start.2
  8.7 0.0 copy-start
  8.7 0.0 copy-start.1
  8.7 0.6 copy-done
  9.4 0.0 copy-done.1
  9.4 3.4 %shard_map.111 = (bf16[128,2048]{1,0:T(8,128)(2,1)S(1)}, bf16[128,2048]{1,0:T(8,128)(2,1)S(1)}, bf16[128,2048]{1,0:T(8,128)(2,1)S(1)}, bf16[128,2048]{1,0:T(8,128)(2,1)S(1)}, f32[16,128]{1,0:T(8,128)S(1)}) custom-call(s32[16]{0:T(128)S(1)} %get-tuple-element.34.prm_ref, bf16[128,2048]{1,0:T(8,128)(2,1)S(1)} %get-tuple-element.35.q_ref.refs_0_, ...), custom_call_target="tpu_custom_call" | custom-call | flops 1073741824 | bytes 4194304 | tf_op jit(solution)/shard_map/pallas_call | solution.py:309
  12.8 4.3 %collective-permute-done.refs_4_ = bf16[576,512]{1,0:T(8,128)(2,1)S(1)} collective-permute-done((bf16[576,512]{1,0:T(8,128)(2,1)S(1)}, bf16[576,512]{1,0:T(8,128)(2,1)S(1)}, u32[]{:S(2)}, u32[]{:S(2)}) %collective-permute-start) | collective-permute-done | bytes 589856 | tf_op jit(solution)/shard_map/ppermute | solution.py:340
  17.1 3.0 %shard_map.112 = (bf16[128,2048]{1,0:T(8,128)(2,1)S(1)}, bf16[128,2048]{1,0:T(8,128)(2,1)S(1)}, bf16[128,2048]{1,0:T(8,128)(2,1)S(1)}, bf16[128,2048]{1,0:T(8,12...) custom-call(s32[16]{0:T(128)S(1)} %get-tuple-element.34.prm_ref, ...), custom_call_target="tpu_custom_call" | custom-call | flops 1073741824 | bytes 4194304 | tf_op jit(solution)/shard_map/pallas_call | solution.py:345
  20.1 0.0 collective-permute-done.2.refs_4_
  20.1 1.0 %shard_map.113 = (bf16[128,2048]{1,0:T(8,128)(2,1)S(1)}, bf16[128,2048]{1,0:T(8,128)(2,1)S(1)}, bf16[128,2048]{1,0:T(8,128)(2,1)S(1)}, bf16[128,2048]{1,0:T(8,12...) custom-call(s32[16]{0:T(128)S(1)} %get-tuple-element.34.prm_ref, ...), custom_call_target="tpu_custom_call" | custom-call | flops 1073741824 | bytes 4194304 | tf_op jit(solution)/shard_map/pallas_call | solution.py:345
  21.0 1.5 %collective-permute-start.3 = (bf16[576,512]{1,0:T(8,128)(2,1)S(1)}, bf16[576,512]{1,0:T(8,128)(2,1)}, u32[]{:S(2)}, u32[]{:S(2)}) collective-permute-start(bf16[576,512]{1,0:T(8,128)(2,1)S(1)} %get-tuple-element.53), channel_id=1, source_target_pairs={{1,2},{3,4},{5,6},{7,8},{9,10},{11,12},{13,14},{2,1},{4,3},{6,5},{... | collective-permute-start | bytes 1769480 | tf_op jit(solution)/shard_map/ppermute | solution.py:357
  22.5 12.8 %collective-permute-start.1 = (bf16[576,512]{1,0:T(8,128)(2,1)S(1)}, bf16[576,512]{1,0:T(8,128)(2,1)}, u32[]{:S(2)}, u32[]{:S(2)}) collective-permute-start(bf16[576,512]{1,0:T(8,128)(2,1)S(1)} %get-tuple-element.46), channel_id=1, source_target_pairs={{0,1},{2,3},{4,5},{6,7},{8,9},{10,11},{12,13},{14,15},{1,0},{3,2},... | collective-permute-start | bytes 1769480 | tf_op jit(solution)/shard_map/ppermute | solution.py:355
  35.4 15.9 %all_to_all.10 = f32[32,2,128]{2,1,0:T(2,128)S(1)} all-to-all(f32[32,2,128]{2,1,0:T(2,128)S(1)} %get-tuple-element.62), channel_id=1, replica_groups=mesh['grp'=32,'tp'=16] {'grp'}, dimensions={0} | all-to-all | bytes 65536 | tf_op jit(solution)/shard_map/all_to_all | solution.py:358
  51.3 0.6 broadcast_in_dim.19
  52.0 13.1 %all-to-all-start.1 = ((f32[16,2,128]{2,1,0:T(2,128)}), f32[16,2,128]{2,1,0:T(2,128)S(1)}, u32[]{:S(2)}, u32[]{:S(2)}) async-start(f32[16,2,128]{2,1,0:T(2,128)} %broadcast_in_dim.19), calls=%async_computation.1 | async-start | bytes 32768 | tf_op jit(solution)/shard_map/all_to_all | solution.py:371
  65.0 0.0 collective-permute-done.3.done2
  65.1 0.0 collective-permute-done.1.done
  65.1 4.1 %shard_map.114 = (bf16[128,2048]{1,0:T(8,128)(2,1)}, bf16[128,2048]{1,0:T(8,128)(2,1)}, bf16[128,2048]{1,0:T(8,128)(2,1)}, bf16[128,2048]{1,0:T(8,128)(2,1)}) custom-call(s32[16]{0:T(128)S(1)} %get-tuple-element.34.prm_ref, bf16[576,512]{1,0:T(8,128)(2,1)} %collective-permute-done.1.done, bf16[576,512]{1,0:T(8,128)(2,1)} %collective-permute-done.3.done2, ...), custom_call_target="tpu_custom_call" | custom-call | flops 1048576 | bytes 4194304 | tf_op jit(solution)/shard_map/pallas_call | solution.py:361
  69.2 7.3 %all-to-all-done.1.parts_ref = f32[16,2,128]{2,1,0:T(2,128)S(1)} async-done(((f32[16,2,128]{2,1,0:T(2,128)}), f32[16,2,128]{2,1,0:T(2,128)S(1)}, u32[]{:S(2)}, u32[]{:S(2)}) %all-to-all-start.1) | async-done | bytes 16416 | tf_op jit(solution)/shard_map/all_to_all | solution.py:371
  76.4 0.6 shard_map.115
  (1 shorter events, 0.0 us)
Async XLA Ops:
  3.3 13.8 %collective-permute-start = (bf16[576,512]{1,0:T(8,128)(2,1)S(1)}, bf16[576,512]{1,0:T(8,128)(2,1)S(1)}, u32[]{:S(2)}, u32[]{:S(2)}) collective-permute-start(bf16[576,512]{1,0:T(8,128)(2,1)S(1)} %get-tuple-element.39), channel_id=1, source_target_pairs={{0,1},{2,3},{4,5},{6,7},{8,9},{10,11},{12,13},{14,15},{1,0},{3,2},... | collective-permute-start | bytes 1769480 | tf_op jit(solution)/shard_map/ppermute | solution.py:340
  8.0 12.1 %collective-permute-start.2 = (bf16[576,512]{1,0:T(8,128)(2,1)S(1)}, bf16[576,512]{1,0:T(8,128)(2,1)S(1)}, u32[]{:S(2)}, u32[]{:S(2)}) collective-permute-start(bf16[576,512]{1,0:T(8,128)(2,1)S(1)} %get-tuple-element.47), channel_id=1, source_target_pairs={{1,2},{3,4},{5,6},{7,8},{9,10},{11,12},{13,14},{2,1},{4,3},{6,5},{... | collective-permute-start | bytes 1769480 | tf_op jit(solution)/shard_map/ppermute | solution.py:341
  8.7 0.7 copy-start
  8.7 0.7 copy-start.1
  21.0 44.0 %collective-permute-start.3 = (bf16[576,512]{1,0:T(8,128)(2,1)S(1)}, bf16[576,512]{1,0:T(8,128)(2,1)}, u32[]{:S(2)}, u32[]{:S(2)}) collective-permute-start(bf16[576,512]{1,0:T(8,128)(2,1)S(1)} %get-tuple-element.53), channel_id=1, source_target_pairs={{1,2},{3,4},{5,6},{7,8},{9,10},{11,12},{13,14},{2,1},{4,3},{6,5},{... | collective-permute-start | bytes 1769480 | tf_op jit(solution)/shard_map/ppermute | solution.py:357
  22.5 42.5 %collective-permute-start.1 = (bf16[576,512]{1,0:T(8,128)(2,1)S(1)}, bf16[576,512]{1,0:T(8,128)(2,1)}, u32[]{:S(2)}, u32[]{:S(2)}) collective-permute-start(bf16[576,512]{1,0:T(8,128)(2,1)S(1)} %get-tuple-element.46), channel_id=1, source_target_pairs={{0,1},{2,3},{4,5},{6,7},{8,9},{10,11},{12,13},{14,15},{1,0},{3,2},... | collective-permute-start | bytes 1769480 | tf_op jit(solution)/shard_map/ppermute | solution.py:355
  52.0 24.5 %all-to-all-start.1 = ((f32[16,2,128]{2,1,0:T(2,128)}), f32[16,2,128]{2,1,0:T(2,128)S(1)}, u32[]{:S(2)}, u32[]{:S(2)}) async-start(f32[16,2,128]{2,1,0:T(2,128)} %broadcast_in_dim.19), calls=%async_computation.1 | async-start | bytes 32768 | tf_op jit(solution)/shard_map/all_to_all | solution.py:371

commit v6 on v5

--- a/solution.py
+++ b/solution.py
@@ -15,6 +15,7 @@
 MOST = 12
 CAP = 36
 SIZE = CAP * BLK
+NONE = -1e30
 MIB = 1024 * 1024
 F32 = jnp.float32
 BF16 = jnp.bfloat16
@@ -54,7 +55,29 @@
     return pl.ds(pl.multiple_of(j * HD, HD), HD)
 
 
-def pack_kernel(heads, q_hbm, k_hbm, v_hbm, g_hbm, seg_hbm, out_ref, out_ref2, prm_ref, q_ref, k_ref, v_ref, g_ref, seg_ref, sem):
+def pack(out_ref, values, refs):
+    is_left, _, _, na, nb, h, rest = values
+    count = jnp.where(is_left == 1, rest, h)
+    blocks = jnp.where(is_left == 1, nb, na)
+    first_head = jnp.where(is_left == 1, h, 0)
+    first_row = jnp.where(is_left == 1, 0, ROWS - na * BLK)
+
+    def head(jj, _):
+        cols = head_cols(first_head + jj)
+
+        def rows(r, _):
+            src = pl.ds(pl.multiple_of(first_row + r * BLK, BLK), BLK)
+            dst = pl.ds(pl.multiple_of((jj * blocks + r) * BLK, BLK), BLK)
+            for t, ref in enumerate(refs):
+                out_ref[dst, t * HD : (t + 1) * HD] = ref[src, cols]
+            return 0
+
+        return lax.fori_loop(0, blocks, rows, 0)
+
+    lax.fori_loop(0, count, head, 0)
+
+
+def pack_kernel(heads, q_hbm, k_hbm, v_hbm, g_hbm, seg_hbm, out_ref, prm_ref, q_ref, k_ref, v_ref, g_ref, seg_ref, sem):
     refs = (q_ref, k_ref, v_ref, g_ref)
     step = ROWS // 4
     copies = []
@@ -70,25 +93,11 @@
     for copy in copies:
         copy.wait()
 
-    for out, (is_left, _, _, na, nb, h, rest) in zip((out_ref, out_ref2), plans):
-        count = jnp.where(is_left == 1, rest, h)
-        blocks = jnp.where(is_left == 1, nb, na)
-        first_head = jnp.where(is_left == 1, h, 0)
-        first_row = jnp.where(is_left == 1, 0, ROWS - na * BLK)
-
-        def head(jj, _):
-            cols = head_cols(first_head + jj)
-
-            def rows(r, _):
-                src = pl.ds(pl.multiple_of(first_row + r * BLK, BLK), BLK)
-                dst = pl.ds(pl.multiple_of((jj * blocks + r) * BLK, BLK), BLK)
-                for t, ref in enumerate(refs):
-                    out[dst, t * HD : (t + 1) * HD] = ref[src, cols]
-                return 0
-
-            return lax.fori_loop(0, blocks, rows, 0)
-
-        lax.fori_loop(0, count, head, 0)
+    pack(out_ref, plans[0], refs)
+
+
+def pack_odd_kernel(prm_ref, q_ref, k_ref, v_ref, g_ref, out_ref):
+    pack(out_ref, [prm_ref[8 + i] for i in range(7)], (q_ref, k_ref, v_ref, g_ref))
 
 
 def mm(x, y, dims):
@@ -108,7 +117,7 @@
 
 def units_attention(items, q_gain, k_gain, scale, mean_of):
     n = range(len(items))
-    q, k, v, g, mask, row_ok = zip(*items)
+    q, k, v, g, bias, row_ok = zip(*items)
 
     def means(x, y):
         both = [mm(jnp.concatenate([x[i].astype(BF16), y[i].astype(BF16)], axis=1), mean_of, NN) for i in n]
@@ -120,9 +129,7 @@
     q_unit, k_unit = [qf[i] * q_recip[i] for i in n], [kf[i] * k_recip[i] for i in n]
     q_norm, k_norm = [(x * q_gain).astype(BF16) for x in q_unit], [(x * k_gain).astype(BF16) for x in k_unit]
     scores = [mm(q_norm[i], k_norm[i], NT) for i in n]
-    weight = [
-        jnp.where(mask[i], jnp.exp2(scores[i] * (scale * math.log2(math.e))), 0.0).astype(BF16) for i in n
-    ]
+    weight = [jnp.exp2(scores[i] * (scale * math.log2(math.e)) + bias[i]).astype(BF16) for i in n]
     ones = jnp.ones((ROWS, HD), BF16)
     sums = [mm(weight[i], jnp.concatenate([v[i], ones], axis=1), NN) for i in n]
     total = [x[:, HD:] for x in sums]
@@ -162,7 +169,7 @@
 def local_kernel(heads, scale, prm_ref, q_ref, k_ref, v_ref, g_ref, seg_ref, qg_ref, kg_ref, o_ref, dq_ref, dk_ref, dv_ref, sums_ref):
     me = lax.axis_index("tp")
     own = jnp.broadcast_to(seg_ref[pl.ds(me, 1), :].astype(F32), (ROWS, ROWS))
-    same = own == own.T
+    same = jnp.where(own == own.T, 0.0, NONE)
     rows = row_ids()
     whole = jnp.logical_and(rows >= prm_ref[7], rows < ROWS - prm_ref[15])
     q_gain, k_gain = qg_ref[...], kg_ref[...]
@@ -218,7 +225,8 @@
             merged = [
                 jnp.where(theirs, in_pad[window, t * HD : (t + 1) * HD], ref[:, cols]) for t, ref in enumerate(own)
             ]
-            items.append((*merged, jnp.logical_and(ok, ok_c), ok))
+            merged[3] = jnp.where(ok, merged[3], jnp.zeros_like(merged[3]))
+            items.append((*merged, jnp.where(ok_c, 0.0, NONE), ok))
             places.append((cols, window, mine))
         results, gq, gk = units_attention(items, q_gain, k_gain, 1.0 / math.sqrt(HD), mean_of)
         for (cols, window, mine), res in zip(places, results):
@@ -328,16 +336,17 @@
     pad = pltpu.VMEM((SIZE + 2 * ROWS, 4 * HD), BF16)
     even, odd = [[(i, i + 1) for i in range(x, ring - 1, 2)] + [(i + 1, i) for i in range(x, ring - 1, 2)] for x in range(2)]
 
-    out, out2, prm, *args, seg = call(
+    out, prm, *args, seg = call(
         functools.partial(pack_kernel, heads),
         [HB] * 5,
-        [VM, VM, SM] + [VM] * 5,
-        [sent, sent, jax.ShapeDtypeStruct((16,), jnp.int32)] + [full] * 4 + [jax.ShapeDtypeStruct(seg.shape, seg.dtype)],
+        [VM, SM] + [VM] * 5,
+        [sent, jax.ShapeDtypeStruct((16,), jnp.int32)] + [full] * 4 + [jax.ShapeDtypeStruct(seg.shape, seg.dtype)],
         1 << 20,
         [pltpu.SemaphoreType.DMA((17,))],
         vmem=12,
     )(*[pltpu.with_memory_space_constraint(x, pltpu.HBM) for x in (*args, seg)])
     received = lax.ppermute(out, "tp", even)
+    out2 = call(pack_odd_kernel, [SM] + [VM] * 4, VM, sent, 1 << 20, vmem=12)(prm, *args)
     received2 = lax.ppermute(out2, "tp", odd)
     *local, sums = local_call(heads, (prm, *args, seg, *gains))
 

time: 77.3 us -> 77.6 us (level)
  waiting for transfers between devices: 11.6 us -> 10.2 us
  blocking collectives: 15.9 us -> 16.8 us
    ppermute x1, waiting for transfers between devices: 4.3 us -> 2.94 us  [per_device(): received = lax.ppermute(out, 'tp', even)]
    all_to_all x1, blocking collectives: 15.9 us -> 16.8 us  [per_device(): sums = jnp.sum(lax.all_to_all(sums, 'grp', 0, 0), axis=0)]
    ppermute x1, starting transfers between devices: 12.8 us -> 13.7 us  [per_device(): done = lax.ppermute(back, 'tp', even)]
    pallas_call x1 -> x2, Pallas kernels: 2.68 us -> 3.04 us  [the longest x1 2.48 us: per_device(): call(functools.partial(pack_kernel, heads), [HB] * 5, [VM, SM] + [VM] * 5...]
where the time goes in v6:
time: 77.6 us; the launch traced here: 77.2 us
  starting transfers between devices  33.2 us (43%)
  blocking collectives  16.8 us (22%)
  Pallas kernels  14.9 us (19%)
  waiting for transfers between devices  10.2 us (13%)
  local copies, waits for them, and re-layouts  1.27 us (2%)
    all_to_all x1, blocking collectives, per_device(): sums = jnp.sum(lax.all_to_all(sums, 'grp', 0, 0), axis=0)  16.8 us
    ppermute x1, starting transfers between devices, per_device(): done = lax.ppermute(back, 'tp', even)  13.7 us
    all_to_all x1, starting transfers between devices, per_device(): sums = lax.all_to_all(jnp.broadcast_to(sums, (ring, 2, HD)), 'tp', 0, 0)  12.9 us
    all_to_all x1, waiting for transfers between devices, per_device(): sums = lax.all_to_all(jnp.broadcast_to(sums, (ring, 2, HD)), 'tp', 0, 0)  7.29 us
    ppermute x1, starting transfers between devices, per_device(): received = lax.ppermute(out, 'tp', even)  4.38 us
    pallas_call x1, Pallas kernels, per_device(): call(functools.partial(merge_kernel, heads), [SM, whole, whole] + [block]...  4.08 us
    pallas_call x2, Pallas kernels, cross(): call(functools.partial(cross_kernel, heads, x), [SM] + [VM] * 12, [VM] *...  3.86 us
    pallas_call x1, Pallas kernels, local_call(): call(functools.partial(local_kernel, heads, 1.0 / math.sqrt(HD)), [SM] +...  3.35 us
  transfers between devices with their start and end apart: 5, of which 2 were waited for; matrix products, arithmetic and copies ran while one was open for 1% of the time, Pallas kernels for 14%

profile of v6, /device:TPU:1, one launch (start us, length us, event | category | flops | bytes accessed | tf_op | source)
XLA Modules:
  0.0 77.2 jit_solution(3109888840108582014)
XLA Ops:
  0.6 2.5 %shard_map.110 = (bf16[576,512]{1,0:T(8,128)(2,1)S(1)}, s32[16]{0:T(128)S(1)}, bf16[128,2048]{1,0:T(8,128)(2,1)S(1)}, bf16[128,2048]{1,0:T(8,128)(2,1)S(1)}, bf1...) custom-call(bf16[128,2048]{1,0:T(8,128)(2,1)} %bitcast.18, ...), custom_call_target="tpu_custom_call" | custom-call | flops 1048576 | bytes 4194304 | tf_op jit(solution)/shard_map/pallas_call | solution.py:339
  3.1 4.4 %collective-permute-start = (bf16[576,512]{1,0:T(8,128)(2,1)S(1)}, bf16[576,512]{1,0:T(8,128)(2,1)S(1)}, u32[]{:S(2)}, u32[]{:S(2)}) collective-permute-start(bf16[576,512]{1,0:T(8,128)(2,1)S(1)} %get-tuple-element.38), channel_id=1, source_target_pairs={{0,1},{2,3},{4,5},{6,7},{8,9},{10,11},{12,13},{14,15},{1,0},{3,2},... | collective-permute-start | bytes 1769480 | tf_op jit(solution)/shard_map/ppermute | solution.py:348
  7.5 0.6 shard_map.113
  8.1 0.7 collective-permute-start.2
  8.8 0.0 copy-start
  8.8 0.0 copy-start.1
  8.8 0.6 copy-done
  9.4 0.0 copy-done.1
  9.4 3.4 %shard_map.111 = (bf16[128,2048]{1,0:T(8,128)(2,1)S(1)}, bf16[128,2048]{1,0:T(8,128)(2,1)S(1)}, bf16[128,2048]{1,0:T(8,128)(2,1)S(1)}, bf16[128,2048]{1,0:T(8,128)(2,1)S(1)}, f32[16,128]{1,0:T(8,128)S(1)}) custom-call(s32[16]{0:T(128)S(1)} %get-tuple-element.33.prm_ref, bf16[128,2048]{1,0:T(8,128)(2,1)S(1)} %get-tuple-element.34.q_ref.refs_0_, ...), custom_call_target="tpu_custom_call" | custom-call | flops 1073741824 | bytes 4194304 | tf_op jit(solution)/shard_map/pallas_call | solution.py:317
  12.8 2.9 %collective-permute-done.refs_4_ = bf16[576,512]{1,0:T(8,128)(2,1)S(1)} collective-permute-done((bf16[576,512]{1,0:T(8,128)(2,1)S(1)}, bf16[576,512]{1,0:T(8,128)(2,1)S(1)}, u32[]{:S(2)}, u32[]{:S(2)}) %collective-permute-start) | collective-permute-done | bytes 589856 | tf_op jit(solution)/shard_map/ppermute | solution.py:348
  15.8 2.9 %shard_map.112 = (bf16[128,2048]{1,0:T(8,128)(2,1)S(1)}, bf16[128,2048]{1,0:T(8,128)(2,1)S(1)}, bf16[128,2048]{1,0:T(8,128)(2,1)S(1)}, bf16[128,2048]{1,0:T(8,12...) custom-call(s32[16]{0:T(128)S(1)} %get-tuple-element.33.prm_ref, ...), custom_call_target="tpu_custom_call" | custom-call | flops 1073741824 | bytes 4194304 | tf_op jit(solution)/shard_map/pallas_call | solution.py:354
  18.6 0.0 collective-permute-done.2.refs_4_
  18.6 1.0 %shard_map.114 = (bf16[128,2048]{1,0:T(8,128)(2,1)S(1)}, bf16[128,2048]{1,0:T(8,128)(2,1)S(1)}, bf16[128,2048]{1,0:T(8,128)(2,1)S(1)}, bf16[128,2048]{1,0:T(8,12...) custom-call(s32[16]{0:T(128)S(1)} %get-tuple-element.33.prm_ref, ...), custom_call_target="tpu_custom_call" | custom-call | flops 1073741824 | bytes 4194304 | tf_op jit(solution)/shard_map/pallas_call | solution.py:354
  19.6 1.5 %collective-permute-start.3 = (bf16[576,512]{1,0:T(8,128)(2,1)S(1)}, bf16[576,512]{1,0:T(8,128)(2,1)}, u32[]{:S(2)}, u32[]{:S(2)}) collective-permute-start(bf16[576,512]{1,0:T(8,128)(2,1)S(1)} %get-tuple-element.51), channel_id=1, source_target_pairs={{1,2},{3,4},{5,6},{7,8},{9,10},{11,12},{13,14},{2,1},{4,3},{6,5},{... | collective-permute-start | bytes 1769480 | tf_op jit(solution)/shard_map/ppermute | solution.py:366
  21.1 13.7 %collective-permute-start.1 = (bf16[576,512]{1,0:T(8,128)(2,1)S(1)}, bf16[576,512]{1,0:T(8,128)(2,1)}, u32[]{:S(2)}, u32[]{:S(2)}) collective-permute-start(bf16[576,512]{1,0:T(8,128)(2,1)S(1)} %get-tuple-element.45), channel_id=1, source_target_pairs={{0,1},{2,3},{4,5},{6,7},{8,9},{10,11},{12,13},{14,15},{1,0},{3,2},... | collective-permute-start | bytes 1769480 | tf_op jit(solution)/shard_map/ppermute | solution.py:364
  34.9 16.8 %all_to_all.10 = f32[32,2,128]{2,1,0:T(2,128)S(1)} all-to-all(f32[32,2,128]{2,1,0:T(2,128)S(1)} %get-tuple-element.60), channel_id=1, replica_groups=mesh['grp'=32,'tp'=16] {'grp'}, dimensions={0} | all-to-all | bytes 65536 | tf_op jit(solution)/shard_map/all_to_all | solution.py:367
  51.7 0.6 broadcast_in_dim.19
  52.3 12.9 %all-to-all-start.1 = ((f32[16,2,128]{2,1,0:T(2,128)}), f32[16,2,128]{2,1,0:T(2,128)S(1)}, u32[]{:S(2)}, u32[]{:S(2)}) async-start(f32[16,2,128]{2,1,0:T(2,128)} %broadcast_in_dim.19), calls=%async_computation.1 | async-start | bytes 32768 | tf_op jit(solution)/shard_map/all_to_all | solution.py:380
  65.3 0.0 collective-permute-done.3.done2
  65.3 0.0 collective-permute-done.1.done
  65.3 4.1 %shard_map.115 = (bf16[128,2048]{1,0:T(8,128)(2,1)}, bf16[128,2048]{1,0:T(8,128)(2,1)}, bf16[128,2048]{1,0:T(8,128)(2,1)}, bf16[128,2048]{1,0:T(8,128)(2,1)}) custom-call(s32[16]{0:T(128)S(1)} %get-tuple-element.33.prm_ref, bf16[576,512]{1,0:T(8,128)(2,1)} %collective-permute-done.1.done, bf16[576,512]{1,0:T(8,128)(2,1)} %collective-permute-done.3.done2, ...), custom_call_target="tpu_custom_call" | custom-call | flops 1048576 | bytes 4194304 | tf_op jit(solution)/shard_map/pallas_call | solution.py:370
  69.4 7.3 %all-to-all-done.1.parts_ref = f32[16,2,128]{2,1,0:T(2,128)S(1)} async-done(((f32[16,2,128]{2,1,0:T(2,128)}), f32[16,2,128]{2,1,0:T(2,128)S(1)}, u32[]{:S(2)}, u32[]{:S(2)}) %all-to-all-start.1) | async-done | bytes 16416 | tf_op jit(solution)/shard_map/all_to_all | solution.py:380
  76.7 0.6 shard_map.116
  (1 shorter events, 0.0 us)
Async XLA Ops:
  3.1 12.6 %collective-permute-start = (bf16[576,512]{1,0:T(8,128)(2,1)S(1)}, bf16[576,512]{1,0:T(8,128)(2,1)S(1)}, u32[]{:S(2)}, u32[]{:S(2)}) collective-permute-start(bf16[576,512]{1,0:T(8,128)(2,1)S(1)} %get-tuple-element.38), channel_id=1, source_target_pairs={{0,1},{2,3},{4,5},{6,7},{8,9},{10,11},{12,13},{14,15},{1,0},{3,2},... | collective-permute-start | bytes 1769480 | tf_op jit(solution)/shard_map/ppermute | solution.py:348
  8.1 10.6 %collective-permute-start.2 = (bf16[576,512]{1,0:T(8,128)(2,1)S(1)}, bf16[576,512]{1,0:T(8,128)(2,1)S(1)}, u32[]{:S(2)}, u32[]{:S(2)}) collective-permute-start(bf16[576,512]{1,0:T(8,128)(2,1)S(1)} %shard_map.113), channel_id=1, source_target_pairs={{1,2},{3,4},{5,6},{7,8},{9,10},{11,12},{13,14},{2,1},{4,3},{6,5},{... | collective-permute-start | bytes 1769480 | tf_op jit(solution)/shard_map/ppermute | solution.py:350
  8.8 0.7 copy-start
  8.8 0.7 copy-start.1
  19.6 45.6 %collective-permute-start.3 = (bf16[576,512]{1,0:T(8,128)(2,1)S(1)}, bf16[576,512]{1,0:T(8,128)(2,1)}, u32[]{:S(2)}, u32[]{:S(2)}) collective-permute-start(bf16[576,512]{1,0:T(8,128)(2,1)S(1)} %get-tuple-element.51), channel_id=1, source_target_pairs={{1,2},{3,4},{5,6},{7,8},{9,10},{11,12},{13,14},{2,1},{4,3},{6,5},{... | collective-permute-start | bytes 1769480 | tf_op jit(solution)/shard_map/ppermute | solution.py:366
  21.1 44.2 %collective-permute-start.1 = (bf16[576,512]{1,0:T(8,128)(2,1)S(1)}, bf16[576,512]{1,0:T(8,128)(2,1)}, u32[]{:S(2)}, u32[]{:S(2)}) collective-permute-start(bf16[576,512]{1,0:T(8,128)(2,1)S(1)} %get-tuple-element.45), channel_id=1, source_target_pairs={{0,1},{2,3},{4,5},{6,7},{8,9},{10,11},{12,13},{14,15},{1,0},{3,2},... | collective-permute-start | bytes 1769480 | tf_op jit(solution)/shard_map/ppermute | solution.py:364
  52.3 24.3 %all-to-all-start.1 = ((f32[16,2,128]{2,1,0:T(2,128)}), f32[16,2,128]{2,1,0:T(2,128)S(1)}, u32[]{:S(2)}, u32[]{:S(2)}) async-start(f32[16,2,128]{2,1,0:T(2,128)} %broadcast_in_dim.19), calls=%async_computation.1 | async-start | bytes 32768 | tf_op jit(solution)/shard_map/all_to_all | solution.py:380
